TPU v7x, 32 devices: a whole 2x2x4 slice. The times are simulated.
32 devices in a mesh: dp: 32 (over z, y, x, core).
Axes of the slice: x: 2, y: 2, z: 4, core: 2. Of those that a mesh axis runs over, the one named last changes fastest.
Arguments:
- layer_in: bfloat16 [4096, 1024], P('dp'), may hold values from -6 to 6
- cotangent: bfloat16 [4096, 1024], P('dp'), may hold values from -6 to 6
- doc_positions: int32 [4096], P('dp'), may hold values from 0 to 2047, as said below
- norm_gain: bfloat16 [1024], P('dp'), may hold values from 0.5 to 1.5
- in_proj: bfloat16 [1024, 3352], P('dp'), may hold values from -0.1875 to 0.1875
- w_query: bfloat16 [1024, 512], P('dp'), may hold values from -0.1875 to 0.1875
- w_key: bfloat16 [1024, 128], P('dp'), may hold values from -0.1875 to 0.1875
- w_value: bfloat16 [1024, 128], P('dp'), may hold values from -0.1875 to 0.1875
- out_proj: bfloat16 [1536, 1024], P(None, 'dp'), may hold values from -0.15625 to 0.15625
- w_attn_out: bfloat16 [512, 1024], P(None, 'dp'), may hold values from -0.75 to 0.75
- ffn_gain: bfloat16 [1024], P('dp'), may hold values from 0.5 to 1.5
- w_gate: bfloat16 [1024, 2048], P('dp'), may hold values from -0.1875 to 0.1875
- w_up: bfloat16 [1024, 2048], P('dp'), may hold values from -0.1875 to 0.1875
- w_down: bfloat16 [2048, 1024], P(None, 'dp'), may hold values from -0.125 to 0.125
- conv_weight: float32 [4, 1792], replicated, may hold values from -3 to 3
- conv_bias: float32 [1792], replicated, may hold values from -3 to 3
- a_log: float32 [24], replicated, may hold values from -7 to 1
- dt_bias: float32 [24], replicated, may hold values from -5 to -2
- d_skip: float32 [24], replicated, may hold values from 0.5 to 1.5
Outputs:
- layer_out: bfloat16 [4096, 1024], P('dp')
- grad_in: float32 [4096, 1024], P('dp')
- grad_norm_gain: float32 [1024], P('dp')
- grad_in_proj: float32 [1024, 3352], P('dp')
- grad_query: float32 [1024, 512], P('dp')
- grad_key: float32 [1024, 128], P('dp')
- grad_value: float32 [1024, 128], P('dp')
- grad_out_proj: float32 [1536, 1024], P(None, 'dp')
- grad_attn_out: float32 [512, 1024], P(None, 'dp')
- grad_ffn_gain: float32 [1024], P('dp')
- grad_gate: float32 [1024, 2048], P('dp')
- grad_up: float32 [1024, 2048], P('dp')
- grad_down: float32 [2048, 1024], P(None, 'dp')
- grad_conv_weight: float32 [4, 1792], replicated
- grad_conv_bias: float32 [1792], replicated
- grad_a_log: float32 [24], replicated
- grad_dt_bias: float32 [24], replicated
- grad_d_skip: float32 [24], replicated
Inputs may be any that keep to these rules, and one draw needn't show every extreme that they name: `doc_positions`: positions count 0, 1, 2, ... along each document. Documents never cross a boundary of the aligned spans of 2048 tokens, and each such span holds one or two documents of 256 to 2048 tokens; in every draw some span is a single document of 2048 tokens.
All inputs are finite; a program needn't handle non-finite values.
Results may differ from a plain program's by a relative error of at most 0.017.
Values may be sent and summed in bfloat16 or wider, within the bound.
No kernel may reach another device: no remote copies, remote signals or barrier semaphores. Data moves between devices by JAX's collectives and lax.ppermute only.
A program may use at most 256 MiB of HBM per device.

v0:
```python
import jax
import jax.numpy as jnp
from jax import lax
from jax.sharding import PartitionSpec as P

MH = 24
HD = 64
NST = 128
KCONV = 4
AH = 8
KVH = 2
SCAN_BLOCK = 128
DI = 1536
CONVCH = 1792
SEQ = 2048


EPS = 1e-05
ROPE_BASE = 10000.0


def passed_along(value, axis, steps):
    count = lax.axis_size(axis)
    first, last = (max(0, -steps), min(count, count - steps))
    return lax.ppermute(value, axis, [(source, source + steps) for source in range(first, last)])


def product(first_arg, second_arg):
    return jnp.dot(first_arg, second_arg, preferred_element_type=jnp.float32)


def times_transposed(first_arg, second_arg):
    return lax.dot_general(
        first_arg, second_arg, (((1,), (1,)), ((), ())), preferred_element_type=jnp.float32
    )


def transposed_times(first_arg, second_arg):
    return lax.dot_general(
        first_arg, second_arg, (((0,), (0,)), ((), ())), preferred_element_type=jnp.float32
    )


def rms_scale(values, gain_vec):
    return values * lax.rsqrt(jnp.mean(values * values, axis=-1, keepdims=True) + EPS) * gain_vec


def rotate(values, positions):
    half_dim = values.shape[-1] // 2
    frequency = ROPE_BASE ** (-jnp.arange(half_dim, dtype=jnp.float32) / half_dim)
    angles = positions.astype(jnp.float32)[:, None] * frequency[None, :]
    cosine = jnp.cos(angles)[:, None, :]
    sine_vals = jnp.sin(angles)[:, None, :]
    first_half = values[..., :half_dim]
    second_half = values[..., half_dim:]
    return jnp.concatenate(
        [
            first_half * cosine - second_half * sine_vals,
            second_half * cosine + first_half * sine_vals,
        ],
        axis=-1,
    )


def causal_conv(padded, conv_weight, conv_bias, positions):
    token_count = padded.shape[0] - (KCONV - 1)
    conv_sum = jnp.zeros((token_count, padded.shape[1]), jnp.float32) + conv_bias[None, :]
    for tap_index in range(KCONV):
        lag_rows = KCONV - 1 - tap_index
        shifted = padded[tap_index : tap_index + token_count] * conv_weight[tap_index][None, :]
        conv_sum = conv_sum + jnp.where((positions >= lag_rows)[:, None], shifted, 0.0)
    return jax.nn.silu(conv_sum)


def scan_blocks(inputs, b_rows, c_rows, step_sizes, log_decay, positions, state_in):
    token_count = inputs.shape[0]
    block_count = token_count // SCAN_BLOCK
    highest = lax.Precision.HIGHEST

    def one_block(state_carry, pieces):
        in_rows, b_part, c_part, step_part, decay_part, pos_part = pieces
        cumulative = jnp.cumsum(decay_part, axis=0)
        row_index = jnp.arange(SCAN_BLOCK)
        doc_start = row_index - pos_part
        inside = (row_index[None, :] <= row_index[:, None]) & (
            row_index[None, :] >= doc_start[:, None]
        )
        log_gap = jnp.where(
            inside[None], cumulative.T[:, :, None] - cumulative.T[:, None, :], -1e30
        )
        inner_sums = jnp.einsum("in,jn->ij", c_part, b_part, precision=highest)
        mixed = jnp.exp(log_gap) * inner_sums[None] * step_part.T[:, None, :]
        local_out = jnp.einsum("hij,jhp->ihp", mixed, in_rows, precision=highest)
        carried = jnp.where((pos_part > row_index)[:, None], jnp.exp(cumulative), 0.0)
        before = (
            jnp.einsum("in,hpn->ihp", c_part, state_carry, precision=highest) * carried[:, :, None]
        )
        last_row = SCAN_BLOCK - 1
        tail_mask = jnp.where(row_index >= last_row - pos_part[last_row], 1.0, 0.0)
        fade_weights = (
            jnp.exp(cumulative[last_row][None, :] - cumulative) * tail_mask[:, None] * step_part
        )
        fresh_state = jnp.einsum("jh,jhp,jn->hpn", fade_weights, in_rows, b_part, precision=highest)
        keep_rate = jnp.where(pos_part[last_row] > last_row, jnp.exp(cumulative[last_row]), 0.0)
        return (keep_rate[:, None, None] * state_carry + fresh_state, local_out + before)

    pieces = (
        inputs.reshape(block_count, SCAN_BLOCK, MH, HD),
        b_rows.reshape(block_count, SCAN_BLOCK, NST),
        c_rows.reshape(block_count, SCAN_BLOCK, NST),
        step_sizes.reshape(block_count, SCAN_BLOCK, MH),
        log_decay.reshape(block_count, SCAN_BLOCK, MH),
        positions.reshape(block_count, SCAN_BLOCK),
    )
    final_state, outputs = lax.scan(jax.checkpoint(one_block), state_in, pieces)
    return (outputs.reshape(token_count, MH, HD), final_state)


def combine_flat(earlier, later):
    rate_earlier = earlier[:MH]
    rate_later = later[:MH]
    state_earlier = earlier[MH:].reshape(MH, -1)
    state_later = later[MH:].reshape(MH, -1)
    joined = state_earlier * rate_later[:, None] + state_later
    return jnp.concatenate([rate_earlier * rate_later, joined.reshape(-1)])


def pack_element(through, state):
    return jnp.concatenate([through, state.reshape(-1)])


def states_forward(element, doublings):
    gathered = element
    strides = [1] + [2**level for level in range(doublings)]
    for index, stride in enumerate(strides):
        arrived = passed_along(gathered.astype(jnp.bfloat16), "dp", stride).astype(gathered.dtype)
        gathered = arrived if index == 0 else combine_flat(arrived, gathered)
    return gathered[MH:].reshape(MH, HD, NST)


def states_backward(element, doublings):
    gathered = element
    strides = [1] + [2**level for level in range(doublings)]
    for index, stride in enumerate(strides):
        arrived = passed_along(gathered.astype(jnp.bfloat16), "dp", -stride).astype(gathered.dtype)
        gathered = arrived if index == 0 else combine_flat(arrived, gathered)
    return gathered[MH:].reshape(MH, HD, NST)


def masked_scores(query_low, window, positions):
    row_count = query_low.shape[0]
    span_rows = window.shape[0]
    grouped = query_low.reshape(row_count, KVH, AH // KVH, HD)
    key_heads = window[:, : KVH * HD].reshape(span_rows, KVH, HD)
    scores = jnp.einsum(
        "sgjd,tgd->gjst", grouped, key_heads, preferred_element_type=jnp.float32
    ) * HD ** (-0.5)
    q_index = span_rows - row_count + jnp.arange(row_count)
    k_index = jnp.arange(span_rows)
    visible = (k_index[None, :] <= q_index[:, None]) & (
        k_index[None, :] >= (q_index - positions)[:, None]
    )
    return (jnp.where(visible, scores, -1e30), grouped, key_heads)


def attend_forward(query_low, window, positions):
    scores, grouped, key_heads = masked_scores(query_low, window, positions)
    totals = jax.nn.logsumexp(scores, axis=-1, keepdims=True)
    weights_low = jnp.exp(scores - totals).astype(jnp.bfloat16)
    value_heads = window[:, KVH * HD :].reshape(window.shape[0], KVH, HD)
    attended = jnp.einsum(
        "gjst,tgd->sgjd", weights_low, value_heads, preferred_element_type=jnp.float32
    )
    return (attended.reshape(query_low.shape[0], AH * HD), totals)


def attend_backward(query_low, window, positions, totals, grad_attended_low):
    scores, grouped, key_heads = masked_scores(query_low, window, positions)
    row_count = query_low.shape[0]
    value_heads = window[:, KVH * HD :].reshape(window.shape[0], KVH, HD)
    weights_full = jnp.exp(scores - totals)
    weights_low = weights_full.astype(jnp.bfloat16)
    grad_grouped = grad_attended_low.reshape(row_count, KVH, AH // KVH, HD)
    grad_weights = jnp.einsum(
        "sgjd,tgd->gjst", grad_grouped, value_heads, preferred_element_type=jnp.float32
    )
    row_sums = jnp.sum(weights_full * grad_weights, axis=-1, keepdims=True)
    grad_scores = (weights_full * (grad_weights - row_sums)).astype(jnp.bfloat16)
    grad_query = jnp.einsum(
        "gjst,tgd->sgjd", grad_scores, key_heads, preferred_element_type=jnp.float32
    ) * HD ** (-0.5)
    grad_keys = jnp.einsum(
        "gjst,sgjd->tgd", grad_scores, grouped, preferred_element_type=jnp.float32
    ) * HD ** (-0.5)
    grad_values = jnp.einsum(
        "gjst,sgjd->tgd", weights_low, grad_grouped, preferred_element_type=jnp.float32
    )
    span_rows = window.shape[0]
    grad_window = jnp.concatenate(
        [grad_keys.reshape(span_rows, KVH * HD), grad_values.reshape(span_rows, KVH * HD)], axis=1
    )
    return (grad_query.reshape(row_count, AH * HD), grad_window)


def body(
    layer_in,
    cotangent,
    doc_positions,
    norm_gain,
    in_proj,
    w_query,
    w_key,
    w_value,
    out_proj,
    w_attn_out,
    ffn_gain,
    w_gate,
    w_up,
    w_down,
    conv_weight,
    conv_bias,
    a_log,
    dt_bias,
    d_skip,
):
    row_count = layer_in.shape[0]
    doublings = (SEQ // row_count).bit_length() - 1
    gain_one, proj_full, query_full, key_full, value_full, out_full, attn_out_full = (
        lax.all_gather(norm_gain, "dp", axis=0, tiled=True),
        lax.all_gather(in_proj, "dp", axis=0, tiled=True),
        lax.all_gather(w_query, "dp", axis=0, tiled=True),
        lax.all_gather(w_key, "dp", axis=0, tiled=True),
        lax.all_gather(w_value, "dp", axis=0, tiled=True),
        lax.all_gather(out_proj, "dp", axis=1, tiled=True),
        lax.all_gather(w_attn_out, "dp", axis=1, tiled=True),
    )
    residual_in = layer_in.astype(jnp.float32)
    normed, norm_back = jax.vjp(rms_scale, residual_in, gain_one.astype(jnp.float32))
    normed_low = normed.astype(jnp.bfloat16)
    projected = product(normed_low, proj_full)
    gate_z = projected[:, :DI]
    conv_low = projected[:, DI : DI + CONVCH].astype(jnp.bfloat16)
    dt_raw = projected[:, DI + CONVCH :]
    rim_rows = passed_along(conv_low[row_count - (KCONV - 1) :], "dp", 1)
    padded = jnp.concatenate([rim_rows, conv_low], axis=0).astype(jnp.float32)

    def mamba_inputs(padded_rows, taps, tap_bias, raw_steps, step_bias, log_rates):
        conv_out = causal_conv(padded_rows, taps, tap_bias, doc_positions)
        step_sizes = jax.nn.softplus(raw_steps + step_bias)
        return (
            conv_out[:, :DI].reshape(row_count, MH, HD),
            conv_out[:, DI : DI + NST],
            conv_out[:, DI + NST :],
            step_sizes,
            -step_sizes * jnp.exp(log_rates),
        )

    (inputs, b_rows, c_rows, step_sizes, log_decay), inputs_back = jax.vjp(
        mamba_inputs, padded, conv_weight, conv_bias, dt_raw, dt_bias, a_log
    )
    cumulative = jnp.cumsum(log_decay, axis=0)
    last_row = row_count - 1
    tail_mask = jnp.where(jnp.arange(row_count) >= last_row - doc_positions[last_row], 1.0, 0.0)
    fade_weights = (
        jnp.exp(cumulative[last_row][None, :] - cumulative) * tail_mask[:, None] * step_sizes
    )
    local_state = jnp.einsum(
        "jh,jhp,jn->hpn", fade_weights, inputs, b_rows, precision=lax.Precision.HIGHEST
    )
    through = jnp.where(doc_positions[last_row] > last_row, jnp.exp(cumulative[last_row]), 0.0)
    state_in = states_forward(pack_element(through, local_state), doublings)

    def mamba_core(
        in_rows, b_part, c_part, step_part, decay_part, start_state, gate_part, skip_part
    ):
        scanned, state_out = scan_blocks(
            in_rows, b_part, c_part, step_part, decay_part, doc_positions, start_state
        )
        mixed = scanned + skip_part[None, :, None] * in_rows
        return (mixed.reshape(row_count, DI) * jax.nn.silu(gate_part), state_out)

    (gated, state_out), core_back = jax.vjp(
        mamba_core, inputs, b_rows, c_rows, step_sizes, log_decay, state_in, gate_z, d_skip
    )
    gated_low = gated.astype(jnp.bfloat16)
    mamba_branch = product(gated_low, out_full)
    query_low = (
        rotate(product(normed_low, query_full).reshape(row_count, AH, HD), doc_positions)
        .reshape(row_count, AH * HD)
        .astype(jnp.bfloat16)
    )
    key_low = (
        rotate(product(normed_low, key_full).reshape(row_count, KVH, HD), doc_positions)
        .reshape(row_count, KVH * HD)
        .astype(jnp.bfloat16)
    )
    value_low = product(normed_low, value_full).astype(jnp.bfloat16)
    window = jnp.concatenate([key_low, value_low], axis=1)
    for doubling in range(doublings):
        arrived = passed_along(window, "dp", 2**doubling)
        window = jnp.concatenate([arrived, window], axis=0)
    attended, totals = attend_forward(query_low, window, doc_positions)
    attended_low = attended.astype(jnp.bfloat16)
    attn_branch = product(attended_low, attn_out_full)
    middle = residual_in + mamba_branch + attn_branch
    gain_two, gate_full, up_full, down_full = (
        lax.all_gather(ffn_gain, "dp", axis=0, tiled=True),
        lax.all_gather(w_gate, "dp", axis=0, tiled=True),
        lax.all_gather(w_up, "dp", axis=0, tiled=True),
        lax.all_gather(w_down, "dp", axis=1, tiled=True),
    )
    normed_two, norm_two_back = jax.vjp(rms_scale, middle, gain_two.astype(jnp.float32))
    normed_two_low = normed_two.astype(jnp.bfloat16)
    gate_value = product(normed_two_low, gate_full)
    up_value = product(normed_two_low, up_full)

    def swiglu(gate_part, up_part):
        return jax.nn.silu(gate_part) * up_part

    activated, swiglu_back = jax.vjp(swiglu, gate_value, up_value)
    hidden_low = activated.astype(jnp.bfloat16)
    layer_out = (middle + product(hidden_low, down_full)).astype(jnp.bfloat16)
    gate_full, up_full, down_full = (gate_full, up_full, down_full)
    grad_top = cotangent.astype(jnp.float32)
    grad_hidden = times_transposed(cotangent, down_full)
    grad_down_full = transposed_times(hidden_low, cotangent)
    grad_gate_value, grad_up_value = swiglu_back(grad_hidden)
    grad_gate_low = grad_gate_value.astype(jnp.bfloat16)
    grad_up_low = grad_up_value.astype(jnp.bfloat16)
    grad_normed_two = times_transposed(grad_gate_low, gate_full) + times_transposed(
        grad_up_low, up_full
    )
    grad_gate_full = transposed_times(normed_two_low, grad_gate_low)
    grad_up_full = transposed_times(normed_two_low, grad_up_low)
    grad_middle_norm, grad_gain_two = norm_two_back(grad_normed_two)
    grad_middle = grad_top + grad_middle_norm
    grad_ffn_gain, grad_gate, grad_up, grad_down = (
        lax.psum_scatter(grad_gain_two, "dp", scatter_dimension=0, tiled=True),
        lax.psum_scatter(grad_gate_full, "dp", scatter_dimension=0, tiled=True),
        lax.psum_scatter(grad_up_full, "dp", scatter_dimension=0, tiled=True),
        lax.psum_scatter(grad_down_full, "dp", scatter_dimension=1, tiled=True),
    )
    proj_full, query_full, key_full, value_full = (proj_full, query_full, key_full, value_full)
    grad_branch_low = grad_middle.astype(jnp.bfloat16)
    grad_gated = times_transposed(grad_branch_low, out_full)
    grad_out_full = transposed_times(gated_low, grad_branch_low)
    grad_attended = times_transposed(grad_branch_low, attn_out_full)
    grad_attn_out_full = transposed_times(attended_low, grad_branch_low)
    grad_query_rot, grad_window = attend_backward(
        query_low, window, doc_positions, totals, grad_attended.astype(jnp.bfloat16)
    )
    for doubling in reversed(range(doublings)):
        half_rows = grad_window.shape[0] // 2
        returned = passed_along(
            grad_window[:half_rows].astype(jnp.bfloat16), "dp", -(2**doubling)
        ).astype(jnp.float32)
        grad_window = grad_window[half_rows:] + returned
    grad_query_raw = (
        rotate(grad_query_rot.reshape(row_count, AH, HD), -doc_positions)
        .reshape(row_count, AH * HD)
        .astype(jnp.bfloat16)
    )
    grad_key_raw = (
        rotate(grad_window[:, : KVH * HD].reshape(row_count, KVH, HD), -doc_positions)
        .reshape(row_count, KVH * HD)
        .astype(jnp.bfloat16)
    )
    grad_value_low = grad_window[:, KVH * HD :].astype(jnp.bfloat16)
    grad_normed = (
        times_transposed(grad_query_raw, query_full)
        + times_transposed(grad_key_raw, key_full)
        + times_transposed(grad_value_low, value_full)
    )
    grad_query_full = transposed_times(normed_low, grad_query_raw)
    grad_key_full = transposed_times(normed_low, grad_key_raw)
    grad_value_full = transposed_times(normed_low, grad_value_low)
    first_terms = core_back((grad_gated, jnp.zeros_like(state_out)))
    grad_state_out = states_backward(pack_element(through, first_terms[5]), doublings)
    second_terms = core_back((jnp.zeros_like(grad_gated), grad_state_out))
    core_terms = jax.tree.map(jnp.add, first_terms, second_terms)
    grad_inputs, grad_b, grad_c, grad_steps, grad_decay, _, grad_gate_z, grad_skip = core_terms
    grad_padded, grad_taps, grad_tap_bias, grad_dt_raw, grad_step_bias, grad_log_rates = (
        inputs_back((grad_inputs, grad_b, grad_c, grad_steps, grad_decay))
    )
    returned_rim = passed_along(grad_padded[: KCONV - 1], "dp", -1)
    grad_conv = grad_padded[KCONV - 1 :]
    grad_conv = jnp.concatenate(
        [grad_conv[: row_count - (KCONV - 1)], grad_conv[row_count - (KCONV - 1) :] + returned_rim],
        axis=0,
    )
    grad_projected_low = jnp.concatenate([grad_gate_z, grad_conv, grad_dt_raw], axis=1).astype(
        jnp.bfloat16
    )
    grad_normed = grad_normed + times_transposed(grad_projected_low, proj_full)
    grad_proj_full = transposed_times(normed_low, grad_projected_low)
    grad_residual_norm, grad_gain_one = norm_back(grad_normed)
    grad_in = grad_middle + grad_residual_norm
    grad_norm_gain, grad_in_proj, grad_query, grad_key, grad_value, grad_out_proj, grad_attn_out = (
        lax.psum_scatter(grad_gain_one, "dp", scatter_dimension=0, tiled=True),
        lax.psum_scatter(grad_proj_full, "dp", scatter_dimension=0, tiled=True),
        lax.psum_scatter(grad_query_full, "dp", scatter_dimension=0, tiled=True),
        lax.psum_scatter(grad_key_full, "dp", scatter_dimension=0, tiled=True),
        lax.psum_scatter(grad_value_full, "dp", scatter_dimension=0, tiled=True),
        lax.psum_scatter(grad_out_full, "dp", scatter_dimension=1, tiled=True),
        lax.psum_scatter(grad_attn_out_full, "dp", scatter_dimension=1, tiled=True),
    )
    grad_conv_weight, grad_conv_bias, grad_a_log, grad_dt_bias, grad_d_skip = lax.psum(
        (grad_taps, grad_tap_bias, grad_log_rates, grad_step_bias, grad_skip), "dp"
    )
    return (
        layer_out,
        grad_in,
        grad_norm_gain,
        grad_in_proj,
        grad_query,
        grad_key,
        grad_value,
        grad_out_proj,
        grad_attn_out,
        grad_ffn_gain,
        grad_gate,
        grad_up,
        grad_down,
        grad_conv_weight,
        grad_conv_bias,
        grad_a_log,
        grad_dt_bias,
        grad_d_skip,
    )


def solution(mesh):
    in_specs = (
        P("dp", None),
        P("dp", None),
        P("dp"),
        P("dp"),
        P("dp", None),
        P("dp", None),
        P("dp", None),
        P("dp", None),
        P(None, "dp"),
        P(None, "dp"),
        P("dp"),
        P("dp", None),
        P("dp", None),
        P(None, "dp"),
        P(),
        P(),
        P(),
        P(),
        P(),
    )
    out_specs = (
        P("dp", None),
        P("dp", None),
        P("dp"),
        P("dp", None),
        P("dp", None),
        P("dp", None),
        P("dp", None),
        P(None, "dp"),
        P(None, "dp"),
        P("dp"),
        P("dp", None),
        P("dp", None),
        P(None, "dp"),
        P(),
        P(),
        P(),
        P(),
        P(),
    )
    return jax.shard_map(body, mesh=mesh, in_specs=in_specs, out_specs=out_specs, check_vma=False)
```

profile of v0, /device:TPU:0, one launch (start us, length us, event | category | flops | bytes accessed | tf_op | source)
XLA Modules:
  0.0 1796.0 jit_solution(5218048022065541117)
XLA Ops:
  12.9 42.1 %all-reduce.20 = (bf16[1024]{0:T(1024)(128)(2,1)S(1)}, bf16[1024]{0:T(1024)(128)(2,1)S(1)}) all-reduce(bf16[1024]{0:T(1024)(128)(2,1)S(1)} %dynamic-update-slice, bf16[1024]{0:T(1024)(128)(2,1)S(1)} %dynamic-update-slice.1), channel_id=1, replica_groups=mesh['dp'=32] {'dp'}, use_global_device_ids=true, to_apply=%add.15 | all-reduce | flops 2048 | bytes 8192
  55.0 41.3 %all_gather.36 = bf16[1024,128]{1,0:T(8,128)(2,1)S(1)} all-gather(bf16[32,128]{1,0:T(8,128)(2,1)} %param.25), channel_id=1, replica_groups=mesh['dp'=32] {'dp'}, dimensions={0}, use_global_device_ids=true | all-gather | bytes 270336 | tf_op jit(solution)/shard_map/all_gather | solution.py:232
  100.9 38.3 %all_gather.37 = bf16[1024,128]{1,0:T(8,128)(2,1)S(1)} all-gather(bf16[32,128]{1,0:T(8,128)(2,1)} %param.26), channel_id=1, replica_groups=mesh['dp'=32] {'dp'}, dimensions={0}, use_global_device_ids=true | all-gather | bytes 270336 | tf_op jit(solution)/shard_map/all_gather | solution.py:233
  143.8 6.3 collective-permute-start.7
  150.2 2.4 collective-permute-done.7
  152.6 5.0 collective-permute-start.8
  161.5 5.4 collective-permute-start.9
  167.2 8.4 collective-permute-done.9
  178.8 4.2 fusion.180
  194.3 2.4 fusion.4
  196.8 4.7 collective-permute-start.2
  205.1 8.8 collective-permute-start.3
  214.2 6.9 collective-permute-done.3
  222.4 9.9 collective-permute-start.4
  232.3 2.5 convolution_convert_fusion.1
  236.3 4.9 collective-permute-done.4
  243.0 8.0 collective-permute-start.5
  251.2 3.2 fusion.20
  257.9 2.5 fusion.29
  264.6 3.9 convolution_add_fusion.5
  272.4 51.8 %all-gather.16.cloned.1.call-done = bf16[1024,2048]{1,0:T(8,128)(2,1)} async-done(((bf16[32,2048]{1,0:T(8,128)(2,1)}), bf16[1024,2048]{1,0:T(8,128)(2,1)}) %all-gather.16.cloned.1.call-update) | async-done | bytes 4194320 | tf_op jit(solution)/shard_map/all_gather | solution.py:308
  324.2 4.0 fusion.181
  328.2 59.4 %all-gather.18.cloned.1.call-done = bf16[1024,2048]{1,0:T(8,128)(2,1)} async-done(((bf16[32,2048]{1,0:T(8,128)(2,1)}), bf16[1024,2048]{1,0:T(8,128)(2,1)}) %all-gather.18.cloned.1.call-update) | async-done | bytes 4194320 | tf_op jit(solution)/shard_map/all_gather | solution.py:309
  387.5 4.0 fusion.182
  391.5 59.5 %all-gather.20.cloned.1.call-done = bf16[2048,1024]{0,1:T(8,128)(2,1)} async-done(((bf16[2048,32]{0,1:T(8,128)(2,1)}), bf16[2048,1024]{0,1:T(8,128)(2,1)}) %all-gather.20.cloned.1.call-update) | async-done | bytes 4194320 | tf_op jit(solution)/shard_map/all_gather | solution.py:310
  451.0 5.0 multiply_convert_fusion
  465.1 6.9 fusion
  472.0 5.4 fusion.146
  477.5 2.3 fusion.2
  483.2 14.7 collective-permute-done.10
  499.4 8.3 collective-permute-done.11
  509.1 5.6 collective-permute-done.12
  521.0 3.2 convolution_multiply_fusion.3
  526.2 2.8 fusion.188
  529.1 4.7 fusion.187
  533.9 5.7 fusion.189
  539.6 5.7 fusion.190
  547.5 5.6 multiply_reduce_fusion.10
  553.1 2.3 copy.321
  568.2 5.5 fusion.52
  589.3 2.3 copy.326
  593.1 5.6 fusion.191
  600.2 4.3 fusion.33
  606.8 2.6 reduce_window_sum.51
  617.8 14.9 collective-permute-done.16
  635.7 11.6 collective-permute-done.17
  654.7 5.7 collective-permute-done.18
  672.9 5.5 fusion.54
  689.8 4.3 fusion.30
  694.0 2.3 copy.334
  696.4 3.0 convolution_bitcast_fusion.1
  699.4 2.6 convolution_bitcast_fusion.3
  713.9 7.1 fusion.105
  722.2 4.5 fusion.40
  727.7 5.5 fusion.106
  733.7 43.9 %all-reduce.19 = (f32[1024]{0:T(1024)S(1)}, f32[1024]{0:T(1024)S(1)}, f32[4,1792]{1,0:T(4,128)}, f32[1792]{0:T(1024)}, f32[24]{0:T(128)}, /*index=5*/f32[24]{0:T(128)}, f32[24]{0:T(128)}) all-reduce(f32[1024]{0:T(1024)S(1)} %get-tuple-element.215, f32[1024]{0:T(1024)S(1)} %copy-done.103, ...), channel_id=2, replica_groups=mesh['dp'=32] {'dp'}, use_global_device_ids=true, to_apply=%region_27.28.clone | all-reduce | flops 11080 | bytes 88640
  779.9 9.3 reduce-scatter.16.cloned.1.call-done
  789.2 135.5 %reduce-scatter.12.cloned.1.call-done = f32[32,512]{1,0:T(8,128)} async-done(((f32[1024,512]{1,0:T(8,128)}), f32[32,512]{1,0:T(8,128)}) %reduce-scatter.12.cloned.1.call-update) | async-done | bytes 65552 | tf_op jit(solution)/shard_map/reduce_scatter | solution.py:401
  924.7 135.5 %reduce-scatter.20.cloned.1.call-done = f32[512,32]{0,1:T(8,128)} async-done(((f32[512,1024]{0,1:T(8,128)}), f32[512,32]{0,1:T(8,128)}) %reduce-scatter.20.cloned.1.call-update) | async-done | bytes 65552 | tf_op jit(solution)/shard_map/reduce_scatter | solution.py:405
  1060.2 116.4 %reduce-scatter.18.cloned.1.call-done = f32[1536,32]{0,1:T(8,128)} async-done(((f32[1536,1024]{0,1:T(8,128)}), f32[1536,32]{0,1:T(8,128)}) %reduce-scatter.18.cloned.1.call-update) | async-done | bytes 196624 | tf_op jit(solution)/shard_map/reduce_scatter | solution.py:404
  1176.6 151.0 %reduce-scatter.22.cloned.1.call-done = f32[32,2048]{1,0:T(8,128)} async-done(((f32[1024,2048]{1,0:T(8,128)}), f32[32,2048]{1,0:T(8,128)}) %reduce-scatter.22.cloned.1.call-update) | async-done | bytes 262160 | tf_op jit(solution)/shard_map/reduce_scatter | solution.py:339
  1327.6 147.6 %reduce-scatter.24.cloned.1.call-done = f32[32,2048]{1,0:T(8,128)} async-done(((f32[1024,2048]{1,0:T(8,128)}), f32[32,2048]{1,0:T(8,128)}) %reduce-scatter.24.cloned.1.call-update) | async-done | bytes 262160 | tf_op jit(solution)/shard_map/reduce_scatter | solution.py:340
  1475.2 147.6 %reduce-scatter.26.cloned.1.call-done = f32[2048,32]{0,1:T(8,128)} async-done(((f32[2048,1024]{0,1:T(8,128)}), f32[2048,32]{0,1:T(8,128)}) %reduce-scatter.26.cloned.1.call-update) | async-done | bytes 262160 | tf_op jit(solution)/shard_map/reduce_scatter | solution.py:341
  1622.8 166.3 %reduce-scatter.10.cloned.1.call-done = f32[32,3352]{1,0:T(8,128)} async-done(((f32[1024,3352]{1,0:T(8,128)}), f32[32,3352]{1,0:T(8,128)}) %reduce-scatter.10.cloned.1.call-update) | async-done | bytes 429072 | tf_op jit(solution)/shard_map/reduce_scatter | solution.py:400
  (583 shorter events, 167.0 us)
Async XLA Ops:
  7.2 142.9 %copy-start.131 = (s32[128]{0:T(128)S(1)}, s32[128]{0:T(128)}, u32[]{:S(2)}) copy-start(s32[128]{0:T(128)} %param.21) | copy-start | bytes 1540
  7.2 150.4 %copy-start.99 = (f32[4,1792]{1,0:T(4,128)S(1)}, f32[4,1792]{1,0:T(4,128)}, u32[]{:S(2)}) copy-start(f32[4,1792]{1,0:T(4,128)} %param.33) | copy-start | bytes 86020
  7.2 152.4 %copy-start.146 = (f32[24]{0:T(128)S(1)}, f32[24]{0:T(128)}, u32[]{:S(2)}) copy-start(f32[24]{0:T(128)} %param.35) | copy-start | bytes 292
  7.2 152.4 %copy-start.145 = (f32[24]{0:T(128)S(1)}, f32[24]{0:T(128)}, u32[]{:S(2)}) copy-start(f32[24]{0:T(128)} %param.37) | copy-start | bytes 292
  7.2 169.6 %all-gather.12.cloned.1.call-start = ((), (), s32[]{:S(2)}) async-start(), calls=%async_computation.11 | async-start | bytes 1081344 | tf_op jit(solution)/shard_map/all_gather | solution.py:231
  8.0 170.9 %all-gather.8.cloned.1.call-start = ((), (), s32[]{:S(2)}) async-start(), calls=%async_computation.9 | async-start | bytes 7299072 | tf_op jit(solution)/shard_map/all_gather | solution.py:230
  8.7 255.9 %all-gather.10.cloned.1.call-start = ((), (), s32[]{:S(2)}) async-start(), calls=%async_computation.10 | async-start | bytes 3244032 | tf_op jit(solution)/shard_map/all_gather | solution.py:234
  9.5 259.1 %all-gather.14.cloned.1.call-start = ((), (), s32[]{:S(2)}) async-start(), calls=%async_computation.12 | async-start | bytes 1081344 | tf_op jit(solution)/shard_map/all_gather | solution.py:235
  10.0 314.1 %all-gather.16.cloned.1.call-start = ((), (), s32[]{:S(2)}) async-start(), calls=%async_computation.13 | async-start | bytes 4325376 | tf_op jit(solution)/shard_map/all_gather | solution.py:308
  10.6 376.9 %all-gather.18.cloned.1.call-start = ((), (), s32[]{:S(2)}) async-start(), calls=%async_computation.14 | async-start | bytes 4325376 | tf_op jit(solution)/shard_map/all_gather | solution.py:309
  11.2 439.8 %all-gather.20.cloned.1.call-start = ((), (), s32[]{:S(2)}) async-start(), calls=%async_computation.15 | async-start | bytes 4325376 | tf_op jit(solution)/shard_map/all_gather | solution.py:310
  96.3 47.4 %copy-start.53 = (bf16[1024,128]{1,0:T(8,128)(2,1)}, bf16[1024,128]{1,0:T(8,128)(2,1)S(1)}, u32[]{:S(2)}) copy-start(bf16[1024,128]{1,0:T(8,128)(2,1)S(1)} %all_gather.36) | copy-start | bytes 786436
  98.1 80.7 %copy-start.92 = (f32[128]{0:T(128)}, f32[128]{0:T(128)S(1)}, u32[]{:S(2)}) copy-start(f32[128]{0:T(128)S(1)} %fusion.131) | copy-start | bytes 1540
  140.6 3.1 collective-permute-start.6
  142.9 637.0 %reduce-scatter.14.cloned.1.call-start = ((), (), s32[]{:S(2)}) async-start(), calls=%async_computation.18 | async-start | bytes 540672 | tf_op jit(solution)/shard_map/reduce_scatter | solution.py:402
  143.8 33.1 %copy-start.2 = (bf16[128,1024]{1,0:T(8,128)(2,1)S(1)}, bf16[128,1024]{1,0:T(8,128)(2,1)}, u32[]{:S(2)}) copy-start(bf16[128,1024]{1,0:T(8,128)(2,1)} %param.19) | copy-start | bytes 786436
  143.8 8.8 collective-permute-start.7
  150.1 36.7 %copy-start.108 = (pred[128]{0:T(512)(128)(4,1)}, pred[128]{0:T(512)(128)(4,1)S(1)}, u32[]{:S(2)}) copy-start(pred[128]{0:T(512)(128)(4,1)S(1)} %get-tuple-element.301) | copy-start | bytes 388
  150.1 36.7 %copy-start.110 = (pred[128]{0:T(512)(128)(4,1)}, pred[128]{0:T(512)(128)(4,1)S(1)}, u32[]{:S(2)}) copy-start(pred[128]{0:T(512)(128)(4,1)S(1)} %get-tuple-element.302) | copy-start | bytes 388
  150.1 36.7 %copy-start.112 = (pred[128]{0:T(512)(128)(4,1)}, pred[128]{0:T(512)(128)(4,1)S(1)}, u32[]{:S(2)}) copy-start(pred[128]{0:T(512)(128)(4,1)S(1)} %get-tuple-element.303) | copy-start | bytes 388
  150.1 36.7 %copy-start.114 = (pred[128]{0:T(512)(128)(4,1)}, pred[128]{0:T(512)(128)(4,1)S(1)}, u32[]{:S(2)}) copy-start(pred[128]{0:T(512)(128)(4,1)S(1)} %get-tuple-element.304) | copy-start | bytes 388
  152.6 8.8 collective-permute-start.8
  157.7 29.2 %copy-start.82 = (f32[1792]{0:T(1024)}, f32[1792]{0:T(1024)S(1)}, u32[]{:S(2)}) copy-start(f32[1792]{0:T(1024)S(1)} %get-tuple-element.217) | copy-start | bytes 21508
  157.7 29.2 %copy-start.84 = (f32[1792]{0:T(1024)}, f32[1792]{0:T(1024)S(1)}, u32[]{:S(2)}) copy-start(f32[1792]{0:T(1024)S(1)} %get-tuple-element.218) | copy-start | bytes 21508
  157.7 29.2 %copy-start.86 = (f32[1792]{0:T(1024)}, f32[1792]{0:T(1024)S(1)}, u32[]{:S(2)}) copy-start(f32[1792]{0:T(1024)S(1)} %get-tuple-element.219) | copy-start | bytes 21508
  157.7 29.2 %copy-start.88 = (f32[1792]{0:T(1024)}, f32[1792]{0:T(1024)S(1)}, u32[]{:S(2)}) copy-start(f32[1792]{0:T(1024)S(1)} %get-tuple-element.220) | copy-start | bytes 21508
  159.6 23.4 %copy-start.136 = (f32[24]{0:T(128)}, f32[24]{0:T(128)S(1)}, u32[]{:S(2)}) copy-start(f32[24]{0:T(128)S(1)} %exp.102) | copy-start | bytes 292
  160.4 300.4 %copy-start.80 = (f32[1024]{0:T(1024)}, f32[1024]{0:T(1024)S(1)}, u32[]{:S(2)}) copy-start(f32[1024]{0:T(1024)S(1)} %convert_element_type.158) | copy-start | bytes 12292
  161.5 14.1 collective-permute-start.9
  167.2 65.1 %copy-start.13 = (pred[128,2048]{0,1:T(8,128)(4,1)}, pred[128,2048]{0,1:T(8,128)(4,1)S(1)}, u32[]{:S(2)}) copy-start(pred[128,2048]{0,1:T(8,128)(4,1)S(1)} %fusion.50) | copy-start | bytes 786436
  184.6 2.1 collective-permute-start
  188.7 62.3 %copy-start.17 = (f32[128,1792]{1,0:T(8,128)}, f32[128,1792]{1,0:T(8,128)S(1)}, u32[]{:S(2)}) copy-start(f32[128,1792]{1,0:T(8,128)S(1)} %get-tuple-element.252) | copy-start | bytes 2752516
  192.1 4.6 collective-permute-start.1
  196.7 35.6 %copy-start = (f32[2,2048,128,4]{2,1,3,0:T(8,128)}, f32[2,2048,128,4]{2,1,3,0:T(8,128)S(1)}, u32[]{:S(2)}) copy-start(f32[2,2048,128,4]{2,1,3,0:T(8,128)S(1)} %get-tuple-element.308) | copy-start | bytes 25165828
  196.8 6.8 collective-permute-start.2
  205.1 16.0 collective-permute-start.3
  222.4 18.7 %collective-permute-start.4 = (bf16[196632]{0:T(1024)(128)(2,1)}, bf16[196632]{0:T(1024)(128)(2,1)}, u32[]{:S(2)}, u32[]{:S(2)}) collective-permute-start(bf16[196632]{0:T(1024)(128)(2,1)} %pad_maximum_fusion.5), channel_id=1, source_target_pairs={{0,4},{1,5},{2,6},{3,7},{4,8},{5,9},{6,10},{7,11},{8,12},{9,13},{1... | collective-permute-start | bytes 1179800 | tf_op jit(solution)/shard_map/ppermute | solution.py:25
  243.0 14.4 collective-permute-start.5
  481.7 36.1 %copy-start.74 = (f32[128,32]{0,1:T(8,128)S(1)}, f32[128,32]{0,1:T(8,128)}, u32[]{:S(2)}) copy-start(f32[128,32]{0,1:T(8,128)} %get-tuple-element.291) | copy-start | bytes 49156
  481.8 36.8 %copy-start.93 = (f32[128]{0:T(128)S(1)}, f32[128]{0:T(128)}, u32[]{:S(2)}) copy-start(f32[128]{0:T(128)} %copy-done.92) | copy-start | bytes 1540
  481.8 16.1 collective-permute-start.10
  498.1 9.6 collective-permute-start.11
  507.8 6.9 collective-permute-start.12
  514.7 3.1 collective-permute-start.13
  519.7 269.5 %reduce-scatter.16.cloned.1.call-start = ((), (), s32[]{:S(2)}) async-start(), calls=%async_computation.19 | async-start | bytes 540672 | tf_op jit(solution)/shard_map/reduce_scatter | solution.py:403
  520.9 403.8 %reduce-scatter.12.cloned.1.call-start = ((), (), s32[]{:S(2)}) async-start(), calls=%async_computation.17 | async-start | bytes 2162688 | tf_op jit(solution)/shard_map/reduce_scatter | solution.py:401
  526.2 534.0 %reduce-scatter.20.cloned.1.call-start = ((), (), s32[]{:S(2)}) async-start(), calls=%async_computation.21 | async-start | bytes 2162688 | tf_op jit(solution)/shard_map/reduce_scatter | solution.py:405
  529.0 647.5 %reduce-scatter.18.cloned.1.call-start = ((), (), s32[]{:S(2)}) async-start(), calls=%async_computation.20 | async-start | bytes 6488064 | tf_op jit(solution)/shard_map/reduce_scatter | solution.py:404
  533.8 793.8 %reduce-scatter.22.cloned.1.call-start = ((), (), s32[]{:S(2)}) async-start(), calls=%async_computation.22 | async-start | bytes 8650752 | tf_op jit(solution)/shard_map/reduce_scatter | solution.py:339
  539.6 935.6 %reduce-scatter.24.cloned.1.call-start = ((), (), s32[]{:S(2)}) async-start(), calls=%async_computation.23 | async-start | bytes 8650752 | tf_op jit(solution)/shard_map/reduce_scatter | solution.py:340
  545.4 1077.4 %reduce-scatter.26.cloned.1.call-start = ((), (), s32[]{:S(2)}) async-start(), calls=%async_computation.24 | async-start | bytes 8650752 | tf_op jit(solution)/shard_map/reduce_scatter | solution.py:341
  588.1 10.7 collective-permute-start.14
  598.8 14.2 collective-permute-start.15
  610.8 1178.3 %reduce-scatter.10.cloned.1.call-start = ((), (), s32[]{:S(2)}) async-start(), calls=%async_computation.16 | async-start | bytes 14598144 | tf_op jit(solution)/shard_map/reduce_scatter | solution.py:400
  614.8 17.9 collective-permute-start.16
  633.2 14.0 collective-permute-start.17
  648.0 12.3 collective-permute-start.18
  707.0 6.0 collective-permute-start.19
  727.7 51.0 %copy-start.142 = (f32[128]{0:T(128)S(1)}, f32[128]{0:T(128)}, u32[]{:S(2)}) copy-start(f32[128]{0:T(128)} %copy-done.141) | copy-start | bytes 1540
  727.7 51.0 %copy-start.27 = (f32[128,1024]{1,0:T(8,128)S(1)}, f32[128,1024]{1,0:T(8,128)}, u32[]{:S(2)}) copy-start(f32[128,1024]{1,0:T(8,128)} %copy-done.26) | copy-start | bytes 1572868
  727.7 51.0 %copy-start.43 = (bf16[128,1024]{1,0:T(8,128)(2,1)S(1)}, bf16[128,1024]{1,0:T(8,128)(2,1)}, u32[]{:S(2)}) copy-start(bf16[128,1024]{1,0:T(8,128)(2,1)} %param.20) | copy-start | bytes 786436
  727.7 51.0 %copy-start.81 = (f32[1024]{0:T(1024)S(1)}, f32[1024]{0:T(1024)}, u32[]{:S(2)}) copy-start(f32[1024]{0:T(1024)} %copy-done.80) | copy-start | bytes 12292
  727.7 51.0 %copy-start.124 = (f32[128]{0:T(128)S(1)}, f32[128]{0:T(128)}, u32[]{:S(2)}) copy-start(f32[128]{0:T(128)} %copy-done.122) | copy-start | bytes 1540
  727.7 51.0 %copy-start.130 = (f32[128]{0:T(128)S(1)}, f32[128]{0:T(128)}, u32[]{:S(2)}) copy-start(f32[128]{0:T(128)} %copy-done.129) | copy-start | bytes 1540
  (122 other events, 640.3 us)
Sparse Core Ops, SparseCore 0:
  10.9 56.4 all-gather.11
  70.3 72.2 all-gather.7
  145.5 58.8 all-gather.9
  207.2 52.9 all-gather.13
  262.9 61.2 all-gather.15
  326.9 60.5 all-gather.17
  390.4 60.5 all-gather.19
  519.8 136.3 reduce-scatter.13
  659.1 130.0 reduce-scatter.15
  791.9 132.7 reduce-scatter.11
  927.6 132.5 reduce-scatter.19
  1066.3 110.2 reduce-scatter.17
  1179.5 148.0 reduce-scatter.21
  1330.4 144.6 reduce-scatter.23
  1478.0 144.7 reduce-scatter.25
  1630.3 158.7 reduce-scatter.9
where the time goes:
time: 1810 us; the launch traced here: 1800 us
  waiting for transfers between devices  1270 us (70%)
  blocking collectives  165 us (9%)
  matrix products  154 us (9%)
  starting transfers between devices  68.2 us (4%)
  local copies, waits for them, and re-layouts  62.8 us (3%)
  other arithmetic  53.9 us (3%)
  between operations  21 us (1%)
    reduce_scatter x1, waiting for transfers between devices, body(): lax.psum_scatter(grad_proj_full, 'dp', scatter_dimension=0, tiled=True)  166 us
    reduce_scatter x1, waiting for transfers between devices, body(): lax.psum_scatter(grad_gate_full, 'dp', scatter_dimension=0, tiled=True)  151 us
    reduce_scatter x1, waiting for transfers between devices, body(): lax.psum_scatter(grad_down_full, 'dp', scatter_dimension=1, tiled=True)  148 us
    reduce_scatter x1, waiting for transfers between devices, body(): lax.psum_scatter(grad_up_full, 'dp', scatter_dimension=0, tiled=True)  148 us
    reduce_scatter x1, waiting for transfers between devices, body(): lax.psum_scatter(grad_attn_out_full, 'dp', scatter_dimension=1, tiled=True)  136 us
    reduce_scatter x1, waiting for transfers between devices, body(): lax.psum_scatter(grad_query_full, 'dp', scatter_dimension=0, tiled=True)  136 us
    reduce_scatter x1, waiting for transfers between devices, body(): lax.psum_scatter(grad_out_full, 'dp', scatter_dimension=1, tiled=True)  116 us
    ppermute x20, waiting for transfers between devices, passed_along(): lax.ppermute(value, axis, [(source, source + steps) for source in range(f...  87.4 us
  transfers between devices with their start and end apart: 36, of which 25 were waited for; matrix products, arithmetic and copies ran while one was open for 13% of the time, Pallas kernels for 0%

commit v1 on v0

v1 whole, which is shorter than its diff:
```python
import jax
import jax.numpy as jnp
from jax import lax
from jax.sharding import PartitionSpec as P

D = 1024
MH = 24
HD = 64
NST = 128
KCONV = 4
AH = 8
KVH = 2
FF = 2048
CHUNK = 128
DI = 1536
CONVCH = 1792
SEQ = 2048

EPS = 1e-05
ROPE_BASE = 10000.0

TEAM = 4
BITS = TEAM.bit_length() - 1
HEADS = MH // TEAM
CX = HEADS * HD
QH = AH // TEAM
CQ = QH * HD
CF = FF // TEAM
SHARE = TEAM // KVH
CB = 2 * NST // TEAM

F32 = jnp.float32
BF16 = jnp.bfloat16


def product(first_arg, second_arg):
    return jnp.dot(first_arg, second_arg, preferred_element_type=F32)


def times_transposed(first_arg, second_arg):
    return lax.dot_general(
        first_arg, second_arg, (((1,), (1,)), ((), ())), preferred_element_type=F32
    )


def transposed_times(first_arg, second_arg):
    return lax.dot_general(
        first_arg, second_arg, (((0,), (0,)), ((), ())), preferred_element_type=F32
    )


def device_index():
    return lax.axis_index("dp")


def member():
    return device_index() % TEAM


def member_bit(bit):
    return (device_index() >> bit) & 1


def peer(value, distance):
    count = lax.axis_size("dp")
    return lax.ppermute(value, "dp", [(i, i ^ distance) for i in range(count)])


def shift_teams(value, steps):
    count = lax.axis_size("dp")
    offset = steps * TEAM
    first, last = (max(0, -offset), min(count, count - offset))
    return lax.ppermute(value, "dp", [(i, i + offset) for i in range(first, last)])


def team_gather(value):
    blocks = value[None]
    for bit in reversed(range(BITS)):
        other = peer(blocks, 1 << bit)
        blocks = jnp.where(
            member_bit(bit) == 0,
            jnp.stack([blocks, other], axis=1),
            jnp.stack([other, blocks], axis=1),
        )
        blocks = blocks.reshape((-1,) + value.shape)
    return blocks.reshape((-1,) + value.shape[1:])


def team_scatter(partial):
    blocks = partial.reshape((TEAM, -1) + partial.shape[1:])
    for bit in range(BITS):
        mine = member_bit(bit)
        halves = blocks.reshape((-1, 2) + blocks.shape[1:])
        kept = lax.dynamic_index_in_dim(halves, mine, 1, False)
        sent = lax.dynamic_index_in_dim(halves, 1 - mine, 1, False)
        blocks = kept.astype(F32) + peer(sent.astype(BF16), 1 << bit).astype(F32)
    return blocks[0]


def member_order(pieces):
    for bit in range(BITS):
        split = pieces.reshape((TEAM >> (bit + 1), 2, 1 << bit) + pieces.shape[1:])
        flipped = jnp.concatenate([split[:, 1:], split[:, :1]], axis=1)
        pieces = jnp.where(member_bit(bit) == 0, split, flipped).reshape(pieces.shape)
    return pieces


def team_exchange(pieces):
    relative = member_order(pieces)
    arrived = [relative[0]] + [peer(relative[k], k) for k in range(1, TEAM)]
    return member_order(jnp.stack(arrived))


def across_groups():
    count = lax.axis_size("dp")
    return [list(range(first, count, TEAM)) for first in range(TEAM)]


def gather_rows(pieces):
    rows = team_exchange(pieces)
    rows = rows.reshape((-1, rows.shape[-1]))
    return lax.all_gather(rows, "dp", axis=0, tiled=True, axis_index_groups=across_groups())


def scatter_rows(matrix):
    summed = lax.psum_scatter(
        matrix, "dp", scatter_dimension=0, tiled=True, axis_index_groups=across_groups()
    )
    return team_exchange(summed.reshape(TEAM, -1, summed.shape[-1]))


def sum_across_teams(vector):
    count = lax.axis_size("dp")
    distance = TEAM
    while distance < count:
        vector = vector + peer(vector, distance)
        distance *= 2
    return vector


def columns_of(matrix, index, width):
    return lax.slice_in_dim(matrix, index * width, (index + 1) * width, axis=1)


def my_slice(array, width, axis=-1):
    axis = axis % array.ndim
    return lax.dynamic_slice_in_dim(array, member() * width, width, axis)


def rotate(values, cosine, sine_vals):
    half_dim = HD // 2
    rows = values.shape[0]
    heads = values.reshape(rows, -1, HD)
    first_half = heads[..., :half_dim]
    second_half = heads[..., half_dim:]
    cosine = cosine[:, None, :]
    sine_vals = sine_vals[:, None, :]
    return jnp.concatenate(
        [
            first_half * cosine - second_half * sine_vals,
            second_half * cosine + first_half * sine_vals,
        ],
        axis=-1,
    ).reshape(values.shape)


def causal_conv(padded, conv_weight, conv_bias, positions):
    token_count = padded.shape[0] - (KCONV - 1)
    conv_sum = jnp.zeros((token_count, padded.shape[1]), F32) + conv_bias[None, :]
    for tap_index in range(KCONV):
        lag_rows = KCONV - 1 - tap_index
        shifted = padded[tap_index : tap_index + token_count] * conv_weight[tap_index][None, :]
        conv_sum = conv_sum + jnp.where((positions >= lag_rows)[:, None], shifted, 0.0)
    return jax.nn.silu(conv_sum)


def ssm_core(inputs, b_rows, c_rows, step_sizes, log_decay, state_in, positions):
    token_count = inputs.shape[0]
    blocks = token_count // CHUNK
    high = lax.Precision.HIGH
    in_rows = inputs.reshape(blocks, CHUNK, HEADS, HD)
    b_part = b_rows.reshape(blocks, CHUNK, NST)
    c_part = c_rows.reshape(blocks, CHUNK, NST)
    step_part = step_sizes.reshape(blocks, CHUNK, HEADS)
    pos_part = positions.reshape(blocks, CHUNK)
    cumulative = jnp.cumsum(log_decay.reshape(blocks, CHUNK, HEADS), axis=1)
    row_index = jnp.arange(CHUNK)
    doc_start = row_index[None, :] - pos_part
    inside = (row_index[None, None, :] <= row_index[None, :, None]) & (
        row_index[None, None, :] >= doc_start[:, :, None]
    )
    by_head = cumulative.transpose(0, 2, 1)
    log_gap = jnp.where(inside[:, None], by_head[:, :, :, None] - by_head[:, :, None, :], -1e30)
    inner_sums = jnp.einsum("cin,cjn->cij", c_part, b_part, precision=high)
    mixed = jnp.exp(log_gap) * inner_sums[:, None] * step_part.transpose(0, 2, 1)[:, :, None, :]
    local_out = jnp.einsum("chij,cjhp->cihp", mixed, in_rows, precision=high)
    last_row = CHUNK - 1
    tail_mask = jnp.where(row_index[None, :] >= last_row - pos_part[:, last_row:], 1.0, 0.0)
    fade_weights = (
        jnp.exp(cumulative[:, last_row:] - cumulative) * tail_mask[:, :, None] * step_part
    )
    fresh = jnp.einsum(
        "cjhp,cjn->chpn", in_rows * fade_weights[..., None], b_part, precision=high
    )
    keep_rate = jnp.where(
        pos_part[:, last_row:] > last_row, jnp.exp(cumulative[:, last_row]), 0.0
    )
    entering = []
    state = state_in
    for block in range(blocks):
        entering.append(state)
        state = keep_rate[block][:, None, None] * state + fresh[block]
    carried = jnp.where(
        (pos_part > row_index[None, :])[:, :, None], jnp.exp(cumulative), 0.0
    )
    before = jnp.einsum("cin,chpn->cihp", c_part, jnp.stack(entering), precision=high)
    outputs = local_out + before * carried[..., None]
    return outputs.reshape(token_count, CX), state


def combine_states(own, rate, steps, reach):
    flat = jnp.concatenate([own.reshape(-1, NST), jnp.broadcast_to(rate[0], (8, NST)),
                            jnp.broadcast_to(rate[1], (8, NST))], axis=0).astype(BF16)
    total = None
    through = None
    for distance in range(1, reach + 1):
        arrived = shift_teams(flat, steps * distance).astype(F32)
        state = arrived[:CX].reshape(HEADS, HD, NST)
        their_rate = (arrived[CX, :HEADS] + arrived[CX + 8, :HEADS])[:, None, None]
        if total is None:
            total, through = state, their_rate
        else:
            total = total + through * state
            through = through * their_rate
    return total


def packed_rate(rate):
    wide = jnp.zeros((NST,), F32).at[:HEADS].set(rate)
    coarse = wide.astype(BF16).astype(F32)
    return coarse, wide - coarse


def masked_scores(query_low, key_low, positions):
    row_count = query_low.shape[0]
    span_rows = key_low.shape[0]
    grouped = query_low.reshape(row_count, QH, HD)
    scores = jnp.einsum("sjd,td->jst", grouped, key_low, preferred_element_type=F32) * HD ** (-0.5)
    q_index = span_rows - row_count + jnp.arange(row_count)
    k_index = jnp.arange(span_rows)
    visible = (k_index[None, :] <= q_index[:, None]) & (
        k_index[None, :] >= (q_index - positions)[:, None]
    )
    return jnp.where(visible, scores, -1e30), grouped


def attend_forward(query_low, key_low, value_low, positions):
    scores, _ = masked_scores(query_low, key_low, positions)
    totals = jax.nn.logsumexp(scores, axis=-1, keepdims=True)
    weights_low = jnp.exp(scores - totals).astype(BF16)
    attended = jnp.einsum("jst,td->sjd", weights_low, value_low, preferred_element_type=F32)
    return attended.reshape(query_low.shape[0], CQ), totals


def attend_backward(query_low, key_low, value_low, positions, totals, grad_attended_low):
    scores, grouped = masked_scores(query_low, key_low, positions)
    row_count = query_low.shape[0]
    weights_full = jnp.exp(scores - totals)
    weights_low = weights_full.astype(BF16)
    grad_grouped = grad_attended_low.reshape(row_count, QH, HD)
    grad_weights = jnp.einsum(
        "sjd,td->jst", grad_grouped, value_low, preferred_element_type=F32
    )
    row_sums = jnp.sum(weights_full * grad_weights, axis=-1, keepdims=True)
    grad_scores = (weights_full * (grad_weights - row_sums)).astype(BF16)
    scale = HD ** (-0.5)
    grad_query = jnp.einsum("jst,td->sjd", grad_scores, key_low, preferred_element_type=F32) * scale
    grad_keys = jnp.einsum("jst,sjd->td", grad_scores, grouped, preferred_element_type=F32) * scale
    grad_values = jnp.einsum("jst,sjd->td", weights_low, grad_grouped, preferred_element_type=F32)
    return grad_query.reshape(row_count, CQ), jnp.concatenate([grad_keys, grad_values], axis=1)


def silu_slope(value):
    chance = jax.nn.sigmoid(value)
    return chance * (1.0 + value * (1.0 - chance))


def body(
    layer_in,
    cotangent,
    doc_positions,
    norm_gain,
    in_proj,
    w_query,
    w_key,
    w_value,
    out_proj,
    w_attn_out,
    ffn_gain,
    w_gate,
    w_up,
    w_down,
    conv_weight,
    conv_bias,
    a_log,
    dt_bias,
    d_skip,
):
    me = member()
    kv_mine = me // SHARE
    bc_cols = in_proj[:, 2 * DI : 2 * DI + 2 * NST]
    dt_cols = in_proj[:, DI + CONVCH :]
    first_pieces = jnp.stack(
        [
            jnp.concatenate(
                [
                    columns_of(in_proj[:, :DI], r, CX),
                    columns_of(in_proj[:, DI : 2 * DI], r, CX),
                    bc_cols,
                    columns_of(w_query, r, CQ),
                    columns_of(w_key, r // SHARE, HD),
                    columns_of(w_value, r // SHARE, HD),
                    columns_of(dt_cols, r, HEADS),
                    norm_gain[:, None],
                ],
                axis=1,
            )
            for r in range(TEAM)
        ]
    )
    out_rows = out_proj.T
    attn_rows = w_attn_out.T
    down_rows = w_down.T
    second_pieces = jnp.stack(
        [
            jnp.concatenate(
                [
                    columns_of(out_rows, r, CX),
                    columns_of(attn_rows, r, CQ),
                    columns_of(w_gate, r, CF),
                    columns_of(w_up, r, CF),
                    columns_of(down_rows, r, CF),
                    ffn_gain[:, None],
                ],
                axis=1,
            )
            for r in range(TEAM)
        ]
    )
    rows_one = gather_rows(first_pieces)
    rows_two = gather_rows(second_pieces)
    team_in = team_gather(layer_in)
    positions = team_gather(doc_positions)
    team_top = team_gather(cotangent)

    z_end = CX
    x_end = 2 * CX
    bc_end = x_end + 2 * NST
    q_end = bc_end + CQ
    kv_end = q_end + 2 * HD
    dt_end = kv_end + HEADS
    main_one = rows_one[:, :dt_end]
    gain_one = rows_one[:, dt_end].astype(F32)
    mix_weights = rows_two[:, : CX + CQ]
    ffn_weights = rows_two[:, CX + CQ : CX + CQ + 2 * CF]
    down_weights = rows_two[:, CX + CQ + 2 * CF : CX + CQ + 3 * CF]
    gain_two = rows_two[:, CX + CQ + 3 * CF].astype(F32)

    tokens = team_in.shape[0]
    row_count = layer_in.shape[0]
    reach = SEQ // tokens - 1
    last = tokens - 1

    wide_in = team_in.astype(F32)
    scaled_in = wide_in * lax.rsqrt(jnp.mean(wide_in * wide_in, axis=-1, keepdims=True) + EPS)
    normed_low = (scaled_in * gain_one).astype(BF16)
    projected = product(normed_low, main_one)

    half_dim = HD // 2
    frequency = ROPE_BASE ** (-jnp.arange(half_dim, dtype=F32) / half_dim)
    angles = positions.astype(F32)[:, None] * frequency[None, :]
    cosine = jnp.cos(angles)
    sine_vals = jnp.sin(angles)

    gate_z = projected[:, :z_end]
    conv_low = projected[:, z_end:bc_end].astype(BF16)
    rim_rows = shift_teams(conv_low[tokens - (KCONV - 1) :], 1)
    query_low = rotate(projected[:, bc_end:q_end], cosine, sine_vals).astype(BF16)
    key_low = rotate(projected[:, q_end : q_end + HD], cosine, sine_vals).astype(BF16)
    value_low = projected[:, q_end + HD : kv_end].astype(BF16)
    dt_raw = projected[:, kv_end:dt_end]
    own_window = jnp.concatenate([key_low, value_low], axis=1)
    window = jnp.concatenate(
        [shift_teams(own_window, steps) for steps in range(reach, 0, -1)] + [own_window], axis=0
    )
    key_window = window[:, :HD]
    value_window = window[:, HD:]

    taps_x = my_slice(conv_weight[:, :DI], CX)
    bias_x = my_slice(conv_bias[:DI], CX)
    taps = jnp.concatenate([taps_x, conv_weight[:, DI:]], axis=1)
    bias = jnp.concatenate([bias_x, conv_bias[DI:]], axis=0)
    my_log_rates = my_slice(a_log, HEADS)
    my_dt_bias = my_slice(dt_bias, HEADS)
    my_skip = my_slice(d_skip, HEADS)
    skip_wide = jnp.repeat(my_skip, HD)

    padded = jnp.concatenate([rim_rows, conv_low], axis=0).astype(F32)
    conv_out = causal_conv(padded, taps, bias, positions)
    inputs = conv_out[:, :CX]
    b_rows = conv_out[:, CX : CX + NST]
    c_rows = conv_out[:, CX + NST :]

    def decays(raw_steps, step_bias, log_rates):
        step_sizes = jax.nn.softplus(raw_steps + step_bias)
        return step_sizes, -step_sizes * jnp.exp(log_rates)

    (step_sizes, log_decay), decays_back = jax.vjp(decays, dt_raw, my_dt_bias, my_log_rates)
    cumulative = jnp.cumsum(log_decay, axis=0)
    row_index = jnp.arange(tokens)
    tail_mask = jnp.where(row_index >= last - positions[last], 1.0, 0.0)
    fade_weights = jnp.exp(cumulative[last][None, :] - cumulative) * tail_mask[:, None] * step_sizes
    local_state = transposed_times(inputs * jnp.repeat(fade_weights, HD, axis=1), b_rows)
    through = jnp.where(positions[last] > last, jnp.exp(cumulative[last]), 0.0)
    rates = packed_rate(through)
    state_in = combine_states(local_state.reshape(HEADS, HD, NST), rates, 1, reach)

    attended, totals = attend_forward(query_low, key_window, value_window, positions)
    attended_low = attended.astype(BF16)

    def core(in_rows, b_part, c_part, step_part, decay_part):
        return ssm_core(in_rows, b_part, c_part, step_part, decay_part, state_in, positions)

    (scanned, _), core_back = jax.vjp(core, inputs, b_rows, c_rows, step_sizes, log_decay)
    ssm_out = scanned + skip_wide * inputs
    silu_z = jax.nn.silu(gate_z)
    gated_low = (ssm_out * silu_z).astype(BF16)
    mixed_low = jnp.concatenate([gated_low, attended_low], axis=1)
    branches = team_scatter(times_transposed(mixed_low, mix_weights))
    middle = layer_in.astype(F32) + branches
    inverse_two = lax.rsqrt(jnp.mean(middle * middle, axis=-1, keepdims=True) + EPS)
    scaled_two = middle * inverse_two
    normed_two = team_gather((scaled_two * gain_two).astype(BF16))
    gate_up = product(normed_two, ffn_weights)
    gate_value = gate_up[:, :CF]
    up_value = gate_up[:, CF:]
    silu_gate = jax.nn.silu(gate_value)
    hidden_low = (silu_gate * up_value).astype(BF16)
    layer_out = (middle + team_scatter(times_transposed(hidden_low, down_weights))).astype(BF16)

    grad_hidden = product(team_top, down_weights)
    grad_gate_up = jnp.concatenate(
        [grad_hidden * up_value * silu_slope(gate_value), grad_hidden * silu_gate], axis=1
    ).astype(BF16)
    grad_normed_two = team_scatter(times_transposed(grad_gate_up, ffn_weights))
    ffn_sums = jnp.concatenate(
        [transposed_times(normed_two, grad_gate_up), transposed_times(team_top, hidden_low)], axis=1
    ).astype(BF16)
    ffn_grads = scatter_rows(ffn_sums)
    grad_gain_two = jnp.sum(grad_normed_two * scaled_two, axis=0)
    pulled = grad_normed_two * gain_two
    grad_middle = cotangent.astype(F32) + inverse_two * (
        pulled - scaled_two * jnp.mean(pulled * scaled_two, axis=-1, keepdims=True)
    )
    grad_branch = team_gather(grad_middle.astype(BF16))
    grad_mixed = product(grad_branch, mix_weights)
    grad_gated = grad_mixed[:, :CX]
    grad_attended_low = grad_mixed[:, CX:].astype(BF16)
    grad_ssm = grad_gated * silu_z
    grad_z_low = (grad_gated * ssm_out * silu_slope(gate_z)).astype(BF16)

    entry_weights = jnp.where((positions > row_index)[:, None], jnp.exp(cumulative), 0.0)
    local_adjoint = transposed_times(grad_ssm * jnp.repeat(entry_weights, HD, axis=1), c_rows)
    grad_state = combine_states(local_adjoint.reshape(HEADS, HD, NST), rates, -1, reach)

    grad_query_rot, grad_window = attend_backward(
        query_low, key_window, value_window, positions, totals, grad_attended_low
    )
    own_grad = grad_window[reach * tokens :]
    for steps in range(1, reach + 1):
        part = grad_window[(reach - steps) * tokens : (reach - steps + 1) * tokens]
        own_grad = own_grad + shift_teams(part.astype(BF16), -steps).astype(F32)
    distance = 1
    while distance < SHARE:
        own_grad = own_grad + peer(own_grad, distance)
        distance *= 2
    grad_query_low = rotate(grad_query_rot, cosine, -sine_vals).astype(BF16)
    grad_key_low = rotate(own_grad[:, :HD], cosine, -sine_vals).astype(BF16)
    grad_value_low = own_grad[:, HD:].astype(BF16)

    grad_core = core_back((grad_ssm, grad_state))
    grad_inputs, grad_b, grad_c, grad_steps, grad_decay = grad_core
    grad_inputs = grad_inputs + skip_wide * grad_ssm
    grad_skip = jnp.sum((grad_ssm * inputs).reshape(tokens, HEADS, HD), axis=(0, 2))
    grad_bc = jnp.concatenate([grad_b, grad_c], axis=1).reshape(tokens, TEAM, CB)
    grad_bc = team_scatter(grad_bc.transpose(1, 0, 2).reshape(TEAM * tokens, CB))
    grad_dt_raw, grad_step_bias, grad_log_rates = decays_back((grad_steps, grad_decay))

    conv_padded = jnp.concatenate([padded[:, :CX], my_slice(padded[:, CX:], CB)], axis=1)
    conv_taps = jnp.concatenate([taps[:, :CX], my_slice(taps[:, CX:], CB)], axis=1)
    conv_shift = jnp.concatenate([bias[:CX], my_slice(bias[CX:], CB)], axis=0)
    _, conv_back = jax.vjp(
        lambda rows, weights, offset: causal_conv(rows, weights, offset, positions),
        conv_padded, conv_taps, conv_shift,
    )
    grad_padded, grad_taps, grad_shift = conv_back(
        jnp.concatenate([grad_inputs, grad_bc], axis=1)
    )
    returned_rim = shift_teams(grad_padded[: KCONV - 1], -1)
    grad_conv = grad_padded[KCONV - 1 :]
    grad_conv = jnp.concatenate(
        [grad_conv[: tokens - (KCONV - 1)], grad_conv[tokens - (KCONV - 1) :] + returned_rim],
        axis=0,
    )
    grad_conv_low = grad_conv.astype(BF16)
    grad_dt_low = grad_dt_raw.astype(BF16)

    early_low = jnp.concatenate([grad_z_low, grad_query_low, grad_key_low, grad_value_low], axis=1)
    mix_sums = jnp.concatenate(
        [
            transposed_times(grad_branch, mixed_low),
            transposed_times(normed_low, early_low),
            grad_gain_two[:, None],
        ],
        axis=1,
    ).astype(BF16)
    mix_grads = scatter_rows(mix_sums)

    shared = 1.0 / SHARE
    late_low = jnp.concatenate([grad_conv_low, grad_dt_low], axis=1)
    all_low = jnp.concatenate(
        [
            grad_z_low,
            grad_conv_low,
            grad_query_low,
            grad_key_low * BF16(shared),
            grad_value_low * BF16(shared),
            grad_dt_low,
        ],
        axis=1,
    )
    back_weights = jnp.concatenate(
        [main_one[:, :x_end], my_slice(main_one[:, x_end:bc_end], CB), main_one[:, bc_end:]], axis=1
    )
    grad_normed_part = times_transposed(all_low, back_weights)
    gain_sums = jnp.sum(grad_normed_part * scaled_in, axis=0)
    late_sums = jnp.concatenate(
        [transposed_times(normed_low, late_low), gain_sums[:, None]], axis=1
    ).astype(BF16)
    late_grads = scatter_rows(late_sums)
    grad_normed = team_scatter(grad_normed_part)
    own_in = layer_in.astype(F32)
    inverse_one = lax.rsqrt(jnp.mean(own_in * own_in, axis=-1, keepdims=True) + EPS)
    own_scaled = own_in * inverse_one
    pulled_one = grad_normed * gain_one
    grad_in = grad_middle + inverse_one * (
        pulled_one - own_scaled * jnp.mean(pulled_one * own_scaled, axis=-1, keepdims=True)
    )

    small = jnp.concatenate(
        [grad_taps.reshape(-1), grad_shift, grad_log_rates, grad_step_bias, grad_skip]
    )
    small = team_gather(sum_across_teams(small)[None])
    width = CX + CB
    taps_all = small[:, : KCONV * width].reshape(TEAM, KCONV, width)
    shift_all = small[:, KCONV * width : (KCONV + 1) * width]
    rest = small[:, (KCONV + 1) * width :].reshape(TEAM, 3, HEADS)
    grad_conv_weight = jnp.concatenate(
        [
            taps_all[:, :, :CX].transpose(1, 0, 2).reshape(KCONV, DI),
            taps_all[:, :, CX:].transpose(1, 0, 2).reshape(KCONV, 2 * NST),
        ],
        axis=1,
    )
    grad_conv_bias = jnp.concatenate([shift_all[:, :CX].reshape(-1), shift_all[:, CX:].reshape(-1)])
    grad_a_log = rest[:, 0].reshape(-1)
    grad_dt_bias = rest[:, 1].reshape(-1)
    grad_d_skip = rest[:, 2].reshape(-1)

    def joined(pieces, first, stop, members=range(TEAM)):
        return jnp.concatenate([pieces[r, :, first:stop] for r in members], axis=1).astype(F32)

    grad_gate = joined(ffn_grads, 0, CF)
    grad_up = joined(ffn_grads, CF, 2 * CF)
    grad_down = joined(ffn_grads, 2 * CF, 3 * CF).T
    grad_out_proj = joined(mix_grads, 0, CX).T
    grad_attn_out = joined(mix_grads, CX, CX + CQ).T
    base = CX + CQ
    owners = range(0, TEAM, SHARE)
    grad_query = joined(mix_grads, base + CX, base + CX + CQ)
    grad_key = joined(mix_grads, base + CX + CQ, base + CX + CQ + HD, owners)
    grad_value = joined(mix_grads, base + CX + CQ + HD, base + CX + CQ + 2 * HD, owners)
    grad_ffn_gain = jnp.sum(mix_grads[:, :, base + CX + CQ + 2 * HD].astype(F32), axis=0)
    grad_in_proj = jnp.concatenate(
        [
            joined(mix_grads, base, base + CX),
            joined(late_grads, 0, CX),
            joined(late_grads, CX, CX + CB),
            joined(late_grads, CX + CB, CX + CB + HEADS),
        ],
        axis=1,
    )
    grad_norm_gain = jnp.sum(late_grads[:, :, CX + CB + HEADS].astype(F32), axis=0)
    return (
        layer_out,
        grad_in,
        grad_norm_gain,
        grad_in_proj,
        grad_query,
        grad_key,
        grad_value,
        grad_out_proj,
        grad_attn_out,
        grad_ffn_gain,
        grad_gate,
        grad_up,
        grad_down,
        grad_conv_weight,
        grad_conv_bias,
        grad_a_log,
        grad_dt_bias,
        grad_d_skip,
    )


def solution(mesh):
    rows = P("dp", None)
    columns = P(None, "dp")
    in_specs = (
        (rows, rows, P("dp"), P("dp"), rows, rows, rows, rows, columns, columns)
        + (P("dp"), rows, rows, columns)
        + (P(),) * 5
    )
    out_specs = (
        (rows, rows, P("dp"), rows, rows, rows, rows, columns, columns)
        + (P("dp"), rows, rows, columns)
        + (P(),) * 5
    )
    return jax.shard_map(body, mesh=mesh, in_specs=in_specs, out_specs=out_specs, check_vma=False)
```

time: 1810 us -> 630 us (0.35)
  waiting for transfers between devices: 1270 us -> 268 us
  blocking collectives: 165 us -> 0 us
  matrix products: 154 us -> 60.3 us
  other arithmetic: 53.9 us -> 102 us
  local copies, waits for them, and re-layouts: 62.8 us -> 85.5 us
    reduce_scatter x9 -> x3, waiting for transfers between devices: 1010 us -> 154 us  [scatter_rows(): lax.psum_scatter(matrix, 'dp', scatter_dimension=0, tiled=True, axis_inde...]
    all_gather x7 -> x2, waiting for transfers between devices: 171 us -> 52.2 us  [gather_rows(): lax.all_gather(rows, 'dp', axis=0, tiled=True, axis_index_groups=across_g...]
    unnamed x2 -> x0, blocking collectives: 85.9 us -> none
    all_gather x2 -> x0, blocking collectives: 79.6 us -> none  [the longest x1 41.3 us: body(): lax.all_gather(w_key, 'dp', axis=0, tiled=True)]
    dot_general x38 -> x22, matrix products: 95.8 us -> 44.7 us  [the longest x4 9.12 us: product(): return jnp.dot(first_arg, second_arg, preferred_element_type=F32)]
    dot_general x9 -> x7, matrix products: 35.8 us -> 8.42 us  [transposed_times(): lax.dot_general(first_arg, second_arg, (((0,), (0,)), ((), ())), preferre...]
    ppermute x20 -> x55, waiting for transfers between devices: 87.4 us -> 62.5 us  [the longest x41 53.7 us: peer(): return lax.ppermute(value, 'dp', [(i, i ^ distance) for i in range(count)])]
    ppermute x20 -> x55, starting transfers between devices: 67.2 us -> 83.3 us  [the longest x14 44.4 us: shift_teams(): lax.ppermute(value, 'dp', [(i, i + offset) for i in range(first, last)])]
  transfers between devices with their start and end apart: 36 -> 60, of which waited for: 25 -> 30; matrix products, arithmetic and copies ran while one was open for 13% -> 32% of each run, Pallas kernels for 0% -> 0%
where the time goes in v1:
time: 630 us; the launch traced here: 620 us
  waiting for transfers between devices  268 us (43%)
  other arithmetic  102 us (16%)
  local copies, waits for them, and re-layouts  85.5 us (14%)
  starting transfers between devices  83.7 us (13%)
  matrix products  60.3 us (10%)
  between operations  19.6 us (3%)
    reduce_scatter x3, waiting for transfers between devices, scatter_rows(): lax.psum_scatter(matrix, 'dp', scatter_dimension=0, tiled=True, axis_inde...  154 us
    ppermute x41, waiting for transfers between devices, peer(): return lax.ppermute(value, 'dp', [(i, i ^ distance) for i in range(count)])  53.7 us
    all_gather x2, waiting for transfers between devices, gather_rows(): lax.all_gather(rows, 'dp', axis=0, tiled=True, axis_index_groups=across_g...  52.2 us
    ppermute x14, starting transfers between devices, shift_teams(): lax.ppermute(value, 'dp', [(i, i + offset) for i in range(first, last)])  44.4 us
    ppermute x41, starting transfers between devices, peer(): return lax.ppermute(value, 'dp', [(i, i ^ distance) for i in range(count)])  38.9 us
    unnamed x446, local copies, waits for them, and re-layouts  22.1 us
  transfers between devices with their start and end apart: 60, of which 30 were waited for; matrix products, arithmetic and copies ran while one was open for 32% of the time, Pallas kernels for 0%

profile of v1, /device:TPU:0, one launch (start us, length us, event | category | flops | bytes accessed | tf_op | source)
XLA Modules:
  0.0 620.0 jit_solution(17546366060364026427)
XLA Ops:
  7.2 3.0 collective-permute-start
  32.9 2.1 fusion.5
  42.3 49.2 %all-gather.3.cloned.1.call-done = bf16[1024,1287]{1,0:T(8,128)(2,1)} async-done(((bf16[128,1287]{1,0:T(8,128)(2,1)}), bf16[1024,1287]{1,0:T(8,128)(2,1)}) %all-gather.3.cloned.1.call-update) | async-done | bytes 2635792 | tf_op jit(solution)/shard_map/all_gather | solution.py:122
  96.5 3.1 collective-permute-start.13
  99.6 3.4 collective-permute-start.12
  103.0 3.8 collective-permute-start.11
  107.0 1.8 reduce-window.6
  112.5 2.7 collective-permute-start.7
  121.7 1.7 divide_multiply_fusion
  124.5 7.8 %collective-permute-start.9 = (bf16[400,128]{1,0:T(8,128)(2,1)}, bf16[400,128]{1,0:T(8,128)(2,1)}, u32[]{:S(2)}, u32[]{:S(2)}) collective-permute-start(bf16[400,128]{1,0:T(8,128)(2,1)} %pad_maximum_fusion.39), channel_id=1, source_target_pairs={{0,8},{1,9},{2,10},{3,11},{4,12},{5,13},{6,14},{7,15},{8,16},{9,17... | collective-permute-start | bytes 307208 | tf_op jit(solution)/shard_map/ppermute | solution.py:73
  132.3 11.0 %collective-permute-start.8 = (bf16[400,128]{1,0:T(8,128)(2,1)}, bf16[400,128]{1,0:T(8,128)(2,1)}, u32[]{:S(2)}, u32[]{:S(2)}) collective-permute-start(bf16[400,128]{1,0:T(8,128)(2,1)} %pad_maximum_fusion.39), channel_id=1, source_target_pairs={{0,4},{1,5},{2,6},{3,7},{4,8},{5,9},{6,10},{7,11},{8,12},{9,13},{1... | collective-permute-start | bytes 307208 | tf_op jit(solution)/shard_map/ppermute | solution.py:73
  148.7 1.7 fusion.78
  150.4 2.4 fusion.231
  152.8 1.8 copy.911
  154.6 3.5 collective-permute-start.10
  167.0 1.9 fusion.36
  169.6 2.5 multiply_convert_fusion.5
  173.2 1.8 fusion.4
  175.0 2.2 exponential_reduce_fusion
  178.3 2.4 convolution_convert_fusion.5
  180.6 3.0 all-gather.5.cloned.1.call-done
  183.7 2.1 fusion.49
  188.0 2.2 collective-permute-done.17
  196.7 6.3 %collective-permute-done.18 = bf16[1,128,1024]{2,1,0:T(8,128)(2,1)} collective-permute-done((bf16[1,128,1024]{2,1,0:T(8,128)(2,1)}, bf16[1,128,1024]{2,1,0:T(8,128)(2,1)}, u32[]{:S(2)}, u32[]{:S(2)}) %collective-permute-start.18) | collective-permute-done | bytes 262176 | tf_op jit(solution)/shard_map/ppermute | solution.py:66
  203.0 1.9 multiply_reduce_fusion.12
  206.6 2.1 collective-permute-done.23
  209.9 3.5 collective-permute-done.19
  215.6 4.0 fusion.11
  227.0 6.6 %collective-permute-done.26 = bf16[1,128,1024]{2,1,0:T(8,128)(2,1)S(1)} collective-permute-done((bf16[1,128,1024]{2,1,0:T(8,128)(2,1)S(1)}, bf16[1,128,1024]{2,1,0:T(8,128)(2,1)S(1)}, u32[]{:S(2)}, u32[]{:S(2)}) %collective-permute-start.26) | collective-permute-done | bytes 262176 | tf_op jit(solution)/shard_map/ppermute | solution.py:66
  234.4 4.0 collective-permute-done.22
  242.0 6.0 collective-permute-done.27
  248.0 1.9 maximum_select_fusion.9
  253.3 2.2 slice.1175
  255.5 2.7 slice.1173
  258.4 5.2 concatenate.631
  269.4 2.4 fusion.47
  280.0 1.9 multiply_reduce_fusion.9
  282.9 3.3 fusion.52
  287.6 6.8 %convolution_bitcast_fusion = f32[2048,64]{0,1:T(8,128)} fusion(bf16[512,2,64]{0,2,1:T(8,128)(2,1)S(1)} %bitcast.816, f32[2048,512,2]{1,0,2:T(8,128)} %copy-done, f32[2,512]{1,0:T(2,128)S(1)} %log_add_fusion, pred[512,2048]{0,1:T(8,128)(4,1)S(1)} %copy-done.5), kind=kOutput, calls=%fused_computation.17 | convolution fusion | flops 276824064 | bytes 10096640 | tf_op jit(solution)/shard_map/jst,sjd->td/dot_general | solution.py:279
  294.5 2.9 fusion
  297.4 2.7 fusion.2
  303.4 1.8 copy.856
  305.2 1.8 concatenate.620
  324.3 2.6 fusion.133
  328.3 1.9 fusion.131
  333.0 2.3 fusion.33
  342.1 5.1 reduce_window_sum.40
  355.2 5.5 multiply_reduce_fusion.7
  363.7 7.7 %collective-permute-done.34 = f32[3,448]{0,1:T(8,128)S(1)} collective-permute-done((f32[3,448]{0,1:T(8,128)S(1)}, f32[3,448]{0,1:T(8,128)S(1)}, u32[]{:S(2)}, u32[]{:S(2)}) %collective-permute-start.34) | collective-permute-done | bytes 5408 | tf_op jit(solution)/shard_map/ppermute | solution.py:73
  373.7 3.0 multiply_reduce_fusion
  382.0 3.0 copy.938
  386.2 3.7 collective-permute-start.50
  391.6 3.4 collective-permute-start.51
  396.6 4.8 collective-permute-start.52
  404.6 3.0 convolution_convert_fusion.2
  412.9 2.2 convolution_convert_fusion.1
  418.3 2.7 copy.936
  421.1 4.9 collective-permute-done.40
  426.2 22.1 %reduce-scatter.10.cloned.1.call-done = bf16[128,455]{1,0:T(8,128)(2,1)} async-done(((bf16[1024,455]{1,0:T(8,128)(2,1)}), bf16[128,455]{1,0:T(8,128)(2,1)}) %reduce-scatter.10.cloned.1.call-update) | async-done | bytes 116496 | tf_op jit(solution)/shard_map/reduce_scatter | solution.py:126
  455.7 69.8 %reduce-scatter.14.cloned.1.call-done = bf16[128,1536]{1,0:T(8,128)(2,1)} async-done(((bf16[1024,1536]{1,0:T(8,128)(2,1)}), bf16[128,1536]{1,0:T(8,128)(2,1)}) %reduce-scatter.14.cloned.1.call-update) | async-done | bytes 393232 | tf_op jit(solution)/shard_map/reduce_scatter | solution.py:126
  530.6 2.5 collective-permute-done.49
  533.1 2.1 collective-permute-done.48
  537.2 61.8 %reduce-scatter.12.cloned.1.call-done = bf16[128,1153]{1,0:T(8,128)(2,1)} async-done(((bf16[1024,1153]{1,0:T(8,128)(2,1)}), bf16[128,1153]{1,0:T(8,128)(2,1)}) %reduce-scatter.12.cloned.1.call-update) | async-done | bytes 295184 | tf_op jit(solution)/shard_map/reduce_scatter | solution.py:126
  603.9 2.2 collective-permute-done.46
  (913 shorter events, 197.1 us)
Async XLA Ops:
  7.2 84.2 %all-gather.3.cloned.1.call-start = ((), (), s32[]{:S(2)}) async-start(), calls=%async_computation.3 | async-start | bytes 3244032 | tf_op jit(solution)/shard_map/all_gather | solution.py:122
  7.2 17.4 %collective-permute-start = (s32[1,128]{1,0:T(1,128)}, s32[1,128]{1,0:T(1,128)S(1)}, u32[]{:S(2)}, u32[]{:S(2)}) collective-permute-start(s32[1,128]{1,0:T(1,128)} %bitcast.888), channel_id=1, source_target_pairs={{0,2},{1,3},{2,0},{3,1},{4,6},{5,7},{6,4},{7,5},{8,10},{9,11},{10,... | collective-permute-start | bytes 1544 | tf_op jit(solution)/shard_map/ppermute | solution.py:66
  10.2 28.2 %collective-permute-start.2 = (bf16[1,128,1024]{2,1,0:T(8,128)(2,1)}, bf16[1,128,1024]{2,1,0:T(8,128)(2,1)S(1)}, u32[]{:S(2)}, u32[]{:S(2)}) collective-permute-start(bf16[1,128,1024]{2,1,0:T(8,128)(2,1)} %bitcast.732), channel_id=1, source_target_pairs={{0,2},{1,3},{2,0},{3,1},{4,6},{5,7},{6,4},{7,5},{8,10},{9,11},{10,... | collective-permute-start | bytes 786440 | tf_op jit(solution)/shard_map/ppermute | solution.py:66
  16.9 13.5 %collective-permute-start.6 = (bf16[32,1287]{1,0:T(8,128)(2,1)S(1)}, bf16[32,1287]{1,0:T(8,128)(2,1)S(1)}, u32[]{:S(2)}, u32[]{:S(2)}) collective-permute-start(bf16[32,1287]{1,0:T(8,128)(2,1)S(1)} %get-tuple-element.152), channel_id=1, source_target_pairs={{0,3},{1,2},{2,1},{3,0},{4,7},{5,6},{6,5},{7,4},{8,11},{9,10},{10,... | collective-permute-start | bytes 247112 | tf_op jit(solution)/shard_map/ppermute | solution.py:66
  17.8 13.2 %collective-permute-start.5 = (bf16[32,1287]{1,0:T(8,128)(2,1)S(1)}, bf16[32,1287]{1,0:T(8,128)(2,1)S(1)}, u32[]{:S(2)}, u32[]{:S(2)}) collective-permute-start(bf16[32,1287]{1,0:T(8,128)(2,1)S(1)} %get-tuple-element.153), channel_id=1, source_target_pairs={{0,2},{1,3},{2,0},{3,1},{4,6},{5,7},{6,4},{7,5},{8,10},{9,11},{10,... | collective-permute-start | bytes 247112 | tf_op jit(solution)/shard_map/ppermute | solution.py:66
  19.0 12.0 %collective-permute-start.4 = (bf16[32,1287]{1,0:T(8,128)(2,1)S(1)}, bf16[32,1287]{1,0:T(8,128)(2,1)S(1)}, u32[]{:S(2)}, u32[]{:S(2)}) collective-permute-start(bf16[32,1287]{1,0:T(8,128)(2,1)S(1)} %get-tuple-element.154), channel_id=1, source_target_pairs={{0,1},{1,0},{2,3},{3,2},{4,5},{5,4},{6,7},{7,6},{8,9},{9,8},{10,11... | collective-permute-start | bytes 247112 | tf_op jit(solution)/shard_map/ppermute | solution.py:66
  19.1 76.0 %copy-start.186 = (f32[32]{0:T(128)}, f32[32]{0:T(128)S(1)}, u32[]{:S(2)}) copy-start(f32[32]{0:T(128)S(1)} %multiply_power_fusion) | copy-start | bytes 388
  22.0 84.9 %copy-start.192 = (f32[6]{0:T(128)}, f32[6]{0:T(128)S(1)}, u32[]{:S(2)}) copy-start(f32[6]{0:T(128)S(1)} %dynamic-slice_exponential_fusion) | copy-start | bytes 76
  24.7 1.4 collective-permute-start.1
  26.0 12.0 %collective-permute-start.16 = (bf16[32,2049]{1,0:T(8,128)(2,1)S(1)}, bf16[32,2049]{1,0:T(8,128)(2,1)S(1)}, u32[]{:S(2)}, u32[]{:S(2)}) collective-permute-start(bf16[32,2049]{1,0:T(8,128)(2,1)S(1)} %get-tuple-element.98), channel_id=1, source_target_pairs={{0,3},{1,2},{2,1},{3,0},{4,7},{5,6},{6,5},{7,4},{8,11},{9,10},{10,... | collective-permute-start | bytes 393416 | tf_op jit(solution)/shard_map/ppermute | solution.py:66
  30.4 86.3 %copy-start.77 = (f32[512,32]{0,1:T(8,128)}, f32[512,32]{0,1:T(8,128)S(1)}, u32[]{:S(2)}) copy-start(f32[512,32]{0,1:T(8,128)S(1)} %get-tuple-element.286) | copy-start | bytes 196612
  30.4 7.6 %collective-permute-start.15 = (bf16[32,2049]{1,0:T(8,128)(2,1)S(1)}, bf16[32,2049]{1,0:T(8,128)(2,1)S(1)}, u32[]{:S(2)}, u32[]{:S(2)}) collective-permute-start(bf16[32,2049]{1,0:T(8,128)(2,1)S(1)} %get-tuple-element.99), channel_id=1, source_target_pairs={{0,2},{1,3},{2,0},{3,1},{4,6},{5,7},{6,4},{7,5},{8,10},{9,11},{10,... | collective-permute-start | bytes 393416 | tf_op jit(solution)/shard_map/ppermute | solution.py:66
  31.0 7.0 %collective-permute-start.14 = (bf16[32,2049]{1,0:T(8,128)(2,1)S(1)}, bf16[32,2049]{1,0:T(8,128)(2,1)S(1)}, u32[]{:S(2)}, u32[]{:S(2)}) collective-permute-start(bf16[32,2049]{1,0:T(8,128)(2,1)S(1)} %get-tuple-element.100), channel_id=1, source_target_pairs={{0,1},{1,0},{2,3},{3,2},{4,5},{5,4},{6,7},{7,6},{8,9},{9,8},{10,11... | collective-permute-start | bytes 393416 | tf_op jit(solution)/shard_map/ppermute | solution.py:66
  32.2 151.4 %all-gather.5.cloned.1.call-start = ((), (), s32[]{:S(2)}) async-start(), calls=%async_computation.4 | async-start | bytes 5013504 | tf_op jit(solution)/shard_map/all_gather | solution.py:122
  39.2 2.1 collective-permute-start.3
  40.9 407.5 %reduce-scatter.10.cloned.1.call-start = ((), (), s32[]{:S(2)}) async-start(), calls=%async_computation.5 | async-start | bytes 1179648 | tf_op jit(solution)/shard_map/reduce_scatter | solution.py:126
  96.5 75.5 %collective-permute-start.13 = (bf16[512,128]{0,1:T(8,128)(2,1)}, bf16[512,128]{0,1:T(8,128)(2,1)}, u32[]{:S(2)}, u32[]{:S(2)}) collective-permute-start(bf16[512,128]{0,1:T(8,128)(2,1)} %pad_maximum_fusion.42), channel_id=1, source_target_pairs={{0,4},{1,5},{2,6},{3,7},{4,8},{5,9},{6,10},{7,11},{8,12},{9,13},{1... | collective-permute-start | bytes 393224 | tf_op jit(solution)/shard_map/ppermute | solution.py:73
  99.6 72.4 %collective-permute-start.12 = (bf16[512,128]{0,1:T(8,128)(2,1)}, bf16[512,128]{0,1:T(8,128)(2,1)}, u32[]{:S(2)}, u32[]{:S(2)}) collective-permute-start(bf16[512,128]{0,1:T(8,128)(2,1)} %pad_maximum_fusion.42), channel_id=1, source_target_pairs={{0,8},{1,9},{2,10},{3,11},{4,12},{5,13},{6,14},{7,15},{8,16},{9,17... | collective-permute-start | bytes 393224 | tf_op jit(solution)/shard_map/ppermute | solution.py:73
  103.0 69.0 %collective-permute-start.11 = (bf16[512,128]{0,1:T(8,128)(2,1)}, bf16[512,128]{0,1:T(8,128)(2,1)}, u32[]{:S(2)}, u32[]{:S(2)}) collective-permute-start(bf16[512,128]{0,1:T(8,128)(2,1)} %pad_maximum_fusion.42), channel_id=1, source_target_pairs={{0,12},{1,13},{2,14},{3,15},{4,16},{5,17},{6,18},{7,19},{8,20},{9,... | collective-permute-start | bytes 393224 | tf_op jit(solution)/shard_map/ppermute | solution.py:73
  112.5 8.7 %collective-permute-start.7 = (bf16[3,640]{0,1:T(8,128)(2,1)S(1)}, bf16[3,640]{0,1:T(8,128)(2,1)S(1)}, u32[]{:S(2)}, u32[]{:S(2)}) collective-permute-start(bf16[3,640]{0,1:T(8,128)(2,1)S(1)} %slice.1069), channel_id=1, source_target_pairs={{0,4},{1,5},{2,6},{3,7},{4,8},{5,9},{6,10},{7,11},{8,12},{9,13},{1... | collective-permute-start | bytes 11528 | tf_op jit(solution)/shard_map/ppermute | solution.py:73
  121.6 142.1 %copy-start.1 = (f32[515,640]{0,1:T(8,128)}, f32[515,640]{0,1:T(8,128)S(1)}, u32[]{:S(2)}) copy-start(f32[515,640]{0,1:T(8,128)S(1)} %maximum_convert_fusion) | copy-start | bytes 3955204
  124.5 34.5 %collective-permute-start.9 = (bf16[400,128]{1,0:T(8,128)(2,1)}, bf16[400,128]{1,0:T(8,128)(2,1)}, u32[]{:S(2)}, u32[]{:S(2)}) collective-permute-start(bf16[400,128]{1,0:T(8,128)(2,1)} %pad_maximum_fusion.39), channel_id=1, source_target_pairs={{0,8},{1,9},{2,10},{3,11},{4,12},{5,13},{6,14},{7,15},{8,16},{9,17... | collective-permute-start | bytes 307208 | tf_op jit(solution)/shard_map/ppermute | solution.py:73
  132.3 22.3 %collective-permute-start.8 = (bf16[400,128]{1,0:T(8,128)(2,1)}, bf16[400,128]{1,0:T(8,128)(2,1)}, u32[]{:S(2)}, u32[]{:S(2)}) collective-permute-start(bf16[400,128]{1,0:T(8,128)(2,1)} %pad_maximum_fusion.39), channel_id=1, source_target_pairs={{0,4},{1,5},{2,6},{3,7},{4,8},{5,9},{6,10},{7,11},{8,12},{9,13},{1... | collective-permute-start | bytes 307208 | tf_op jit(solution)/shard_map/ppermute | solution.py:73
  154.6 8.6 %collective-permute-start.10 = (bf16[400,128]{1,0:T(8,128)(2,1)}, bf16[400,128]{1,0:T(8,128)(2,1)S(1)}, u32[]{:S(2)}, u32[]{:S(2)}) collective-permute-start(bf16[400,128]{1,0:T(8,128)(2,1)} %pad_maximum_fusion.39), channel_id=1, source_target_pairs={{0,12},{1,13},{2,14},{3,15},{4,16},{5,17},{6,18},{7,19},{8,20},{9,... | collective-permute-start | bytes 307208 | tf_op jit(solution)/shard_map/ppermute | solution.py:73
  188.0 2.3 collective-permute-start.17
  193.6 9.5 %collective-permute-start.18 = (bf16[1,128,1024]{2,1,0:T(8,128)(2,1)}, bf16[1,128,1024]{2,1,0:T(8,128)(2,1)}, u32[]{:S(2)}, u32[]{:S(2)}) collective-permute-start(bf16[1,128,1024]{2,1,0:T(8,128)(2,1)} %dynamic-slice_convert_fusion.3), channel_id=1, source_target_pairs={{0,2},{1,3},{2,0},{3,1},{4,6},{5,7},{6,4},{7,5},{8,10},{9,11},{10,... | collective-permute-start | bytes 786440 | tf_op jit(solution)/shard_map/ppermute | solution.py:66
  195.1 13.6 %collective-permute-start.23 = (bf16[1,128,1024]{2,1,0:T(8,128)(2,1)S(1)}, bf16[1,128,1024]{2,1,0:T(8,128)(2,1)}, u32[]{:S(2)}, u32[]{:S(2)}) collective-permute-start(bf16[1,128,1024]{2,1,0:T(8,128)(2,1)S(1)} %bitcast.759), channel_id=1, source_target_pairs={{0,2},{1,3},{2,0},{3,1},{4,6},{5,7},{6,4},{7,5},{8,10},{9,11},{10,... | collective-permute-start | bytes 786440 | tf_op jit(solution)/shard_map/ppermute | solution.py:66
  205.0 8.3 %collective-permute-start.19 = (bf16[1,128,1024]{2,1,0:T(8,128)(2,1)S(1)}, bf16[1,128,1024]{2,1,0:T(8,128)(2,1)S(1)}, u32[]{:S(2)}, u32[]{:S(2)}) collective-permute-start(bf16[1,128,1024]{2,1,0:T(8,128)(2,1)S(1)} %get-tuple-element.108), channel_id=1, source_target_pairs={{0,2},{1,3},{2,0},{3,1},{4,6},{5,7},{6,4},{7,5},{8,10},{9,11},{10,... | collective-permute-start | bytes 786440 | tf_op jit(solution)/shard_map/ppermute | solution.py:66
  209.8 4.9 collective-permute-start.24
  213.5 2.0 collective-permute-start.20
  222.2 2.0 collective-permute-start.25
  223.1 2.8 collective-permute-start.21
  224.3 9.2 %collective-permute-start.26 = (bf16[1,128,1024]{2,1,0:T(8,128)(2,1)S(1)}, bf16[1,128,1024]{2,1,0:T(8,128)(2,1)S(1)}, u32[]{:S(2)}, u32[]{:S(2)}) collective-permute-start(bf16[1,128,1024]{2,1,0:T(8,128)(2,1)S(1)} %dynamic-slice_convert_fusion.1), channel_id=1, source_target_pairs={{0,2},{1,3},{2,0},{3,1},{4,6},{5,7},{6,4},{7,5},{8,10},{9,11},{10,... | collective-permute-start | bytes 786440 | tf_op jit(solution)/shard_map/ppermute | solution.py:66
  226.1 12.2 %collective-permute-start.22 = (bf16[1,128,1024]{2,1,0:T(8,128)(2,1)S(1)}, bf16[1,128,1024]{2,1,0:T(8,128)(2,1)S(1)}, u32[]{:S(2)}, u32[]{:S(2)}) collective-permute-start(bf16[1,128,1024]{2,1,0:T(8,128)(2,1)S(1)} %dynamic-slice_convert_fusion.2), channel_id=1, source_target_pairs={{0,2},{1,3},{2,0},{3,1},{4,6},{5,7},{6,4},{7,5},{8,10},{9,11},{10,... | collective-permute-start | bytes 786440 | tf_op jit(solution)/shard_map/ppermute | solution.py:66
  240.3 7.7 %collective-permute-start.27 = (bf16[1,128,1024]{2,1,0:T(8,128)(2,1)S(1)}, bf16[1,128,1024]{2,1,0:T(8,128)(2,1)}, u32[]{:S(2)}, u32[]{:S(2)}) collective-permute-start(bf16[1,128,1024]{2,1,0:T(8,128)(2,1)S(1)} %convert_bitcast_fusion.2), channel_id=1, source_target_pairs={{0,2},{1,3},{2,0},{3,1},{4,6},{5,7},{6,4},{7,5},{8,10},{9,11},{10,... | collective-permute-start | bytes 786440 | tf_op jit(solution)/shard_map/ppermute | solution.py:66
  249.9 17.0 %collective-permute-start.28 = (bf16[2,128,1024]{2,1,0:T(8,128)(2,1)}, bf16[2,128,1024]{2,1,0:T(8,128)(2,1)}, u32[]{:S(2)}, u32[]{:S(2)}) collective-permute-start(bf16[2,128,1024]{2,1,0:T(8,128)(2,1)} %maximum_select_fusion.9), channel_id=1, source_target_pairs={{0,1},{1,0},{2,3},{3,2},{4,5},{5,4},{6,7},{7,6},{8,9},{9,8},{10,11... | collective-permute-start | bytes 1572872 | tf_op jit(solution)/shard_map/ppermute | solution.py:66
  275.8 42.4 %collective-permute-start.31 = (bf16[400,128]{1,0:T(8,128)(2,1)}, bf16[400,128]{1,0:T(8,128)(2,1)}, u32[]{:S(2)}, u32[]{:S(2)}) collective-permute-start(bf16[400,128]{1,0:T(8,128)(2,1)} %pad_maximum_fusion.38), channel_id=1, source_target_pairs={{12,0},{13,1},{14,2},{15,3},{16,4},{17,5},{18,6},{19,7},{20,8},{21... | collective-permute-start | bytes 307208 | tf_op jit(solution)/shard_map/ppermute | solution.py:73
  277.1 37.5 %collective-permute-start.30 = (bf16[400,128]{1,0:T(8,128)(2,1)}, bf16[400,128]{1,0:T(8,128)(2,1)}, u32[]{:S(2)}, u32[]{:S(2)}) collective-permute-start(bf16[400,128]{1,0:T(8,128)(2,1)} %pad_maximum_fusion.38), channel_id=1, source_target_pairs={{8,0},{9,1},{10,2},{11,3},{12,4},{13,5},{14,6},{15,7},{16,8},{17,9... | collective-permute-start | bytes 307208 | tf_op jit(solution)/shard_map/ppermute | solution.py:73
  278.4 33.8 %collective-permute-start.29 = (bf16[400,128]{1,0:T(8,128)(2,1)}, bf16[400,128]{1,0:T(8,128)(2,1)}, u32[]{:S(2)}, u32[]{:S(2)}) collective-permute-start(bf16[400,128]{1,0:T(8,128)(2,1)} %pad_maximum_fusion.38), channel_id=1, source_target_pairs={{4,0},{5,1},{6,2},{7,3},{8,4},{9,5},{10,6},{11,7},{12,8},{13,9},{1... | collective-permute-start | bytes 307208 | tf_op jit(solution)/shard_map/ppermute | solution.py:73
  308.9 43.5 %collective-permute-start.35 = (bf16[512,128]{0,1:T(8,128)(2,1)}, bf16[512,128]{0,1:T(8,128)(2,1)}, u32[]{:S(2)}, u32[]{:S(2)}) collective-permute-start(bf16[512,128]{0,1:T(8,128)(2,1)} %get-tuple-element.109), channel_id=1, source_target_pairs={{4,0},{5,1},{6,2},{7,3},{8,4},{9,5},{10,6},{11,7},{12,8},{13,9},{1... | collective-permute-start | bytes 393224 | tf_op jit(solution)/shard_map/ppermute | solution.py:73
  310.2 42.2 %collective-permute-start.37 = (bf16[512,128]{0,1:T(8,128)(2,1)}, bf16[512,128]{0,1:T(8,128)(2,1)}, u32[]{:S(2)}, u32[]{:S(2)}) collective-permute-start(bf16[512,128]{0,1:T(8,128)(2,1)} %get-tuple-element.110), channel_id=1, source_target_pairs={{12,0},{13,1},{14,2},{15,3},{16,4},{17,5},{18,6},{19,7},{20,8},{21... | collective-permute-start | bytes 393224 | tf_op jit(solution)/shard_map/ppermute | solution.py:73
  312.2 40.2 %collective-permute-start.36 = (bf16[512,128]{0,1:T(8,128)(2,1)}, bf16[512,128]{0,1:T(8,128)(2,1)}, u32[]{:S(2)}, u32[]{:S(2)}) collective-permute-start(bf16[512,128]{0,1:T(8,128)(2,1)} %get-tuple-element.111), channel_id=1, source_target_pairs={{8,0},{9,1},{10,2},{11,3},{12,4},{13,5},{14,6},{15,7},{16,8},{17,9... | collective-permute-start | bytes 393224 | tf_op jit(solution)/shard_map/ppermute | solution.py:73
  339.2 10.5 %collective-permute-start.32 = (bf16[2,512,64]{1,2,0:T(8,128)(2,1)S(1)}, bf16[2,512,64]{1,2,0:T(8,128)(2,1)}, u32[]{:S(2)}, u32[]{:S(2)}) collective-permute-start(bf16[2,512,64]{1,2,0:T(8,128)(2,1)S(1)} %fusion.136), channel_id=1, source_target_pairs={{0,1},{1,0},{2,3},{3,2},{4,5},{5,4},{6,7},{7,6},{8,9},{9,8},{10,11... | collective-permute-start | bytes 393224 | tf_op jit(solution)/shard_map/ppermute | solution.py:66
  350.8 4.3 collective-permute-start.33
  353.6 18.2 %collective-permute-start.38 = (f32[512,128]{0,1:T(8,128)S(1)}, f32[512,128]{0,1:T(8,128)S(1)}, u32[]{:S(2)}, u32[]{:S(2)}) collective-permute-start(f32[512,128]{0,1:T(8,128)S(1)} %fusion.123), channel_id=1, source_target_pairs={{0,1},{1,0},{2,3},{3,2},{4,5},{5,4},{6,7},{7,6},{8,9},{9,8},{10,11... | collective-permute-start | bytes 786440 | tf_op jit(solution)/shard_map/ppermute | solution.py:66
  361.2 10.2 %collective-permute-start.34 = (f32[3,448]{0,1:T(8,128)S(1)}, f32[3,448]{0,1:T(8,128)S(1)}, u32[]{:S(2)}, u32[]{:S(2)}) collective-permute-start(f32[3,448]{0,1:T(8,128)S(1)} %pad_add_fusion.4), channel_id=1, source_target_pairs={{4,0},{5,1},{6,2},{7,3},{8,4},{9,5},{10,6},{11,7},{12,8},{13,9},{1... | collective-permute-start | bytes 16136 | tf_op jit(solution)/shard_map/ppermute | solution.py:73
  378.9 146.5 %reduce-scatter.14.cloned.1.call-start = ((), (), s32[]{:S(2)}) async-start(), calls=%async_computation.7 | async-start | bytes 3538944 | tf_op jit(solution)/shard_map/reduce_scatter | solution.py:126
  385.1 213.8 %reduce-scatter.12.cloned.1.call-start = ((), (), s32[]{:S(2)}) async-start(), calls=%async_computation.6 | async-start | bytes 2949120 | tf_op jit(solution)/shard_map/reduce_scatter | solution.py:126
  386.2 5.4 collective-permute-start.50
  391.6 5.0 collective-permute-start.51
  396.6 6.5 %collective-permute-start.52 = (f32[2258]{0:T(1024)S(1)}, f32[2258]{0:T(1024)S(1)}, u32[]{:S(2)}, u32[]{:S(2)}) collective-permute-start(f32[2258]{0:T(1024)S(1)} %add.559), channel_id=1, source_target_pairs={{0,16},{1,17},{2,18},{3,19},{4,20},{5,21},{6,22},{7,23},{8,24},{9,... | collective-permute-start | bytes 27104 | tf_op jit(solution)/shard_map/ppermute | solution.py:66
  403.1 4.5 collective-permute-start.53
  407.7 1.3 collective-permute-start.54
  410.2 5.0 collective-permute-start.39
  417.5 8.5 %collective-permute-start.40 = (bf16[1,128,1024]{2,1,0:T(8,128)(2,1)S(1)}, bf16[1,128,1024]{2,1,0:T(8,128)(2,1)S(1)}, u32[]{:S(2)}, u32[]{:S(2)}) collective-permute-start(bf16[1,128,1024]{2,1,0:T(8,128)(2,1)S(1)} %dynamic-slice_convert_fusion), channel_id=1, source_target_pairs={{0,2},{1,3},{2,0},{3,1},{4,6},{5,7},{6,4},{7,5},{8,10},{9,11},{10,... | collective-permute-start | bytes 786440 | tf_op jit(solution)/shard_map/ppermute | solution.py:66
  451.2 3.7 collective-permute-start.43
  451.3 4.0 collective-permute-start.42
  452.8 2.5 collective-permute-start.41
  528.0 5.1 collective-permute-start.49
  528.3 7.0 %collective-permute-start.48 = (bf16[32,1536]{1,0:T(8,128)(2,1)S(1)}, bf16[32,1536]{1,0:T(8,128)(2,1)S(1)}, u32[]{:S(2)}, u32[]{:S(2)}) collective-permute-start(bf16[32,1536]{1,0:T(8,128)(2,1)S(1)} %get-tuple-element.133), channel_id=1, source_target_pairs={{0,2},{1,3},{2,0},{3,1},{4,6},{5,7},{6,4},{7,5},{8,10},{9,11},{10,... | collective-permute-start | bytes 294920 | tf_op jit(solution)/shard_map/ppermute | solution.py:66
  529.6 5.6 collective-permute-start.47
  601.3 4.8 collective-permute-start.46
  601.4 6.2 %collective-permute-start.45 = (bf16[32,1153]{1,0:T(8,128)(2,1)S(1)}, bf16[32,1153]{1,0:T(8,128)(2,1)S(1)}, u32[]{:S(2)}, u32[]{:S(2)}) collective-permute-start(bf16[32,1153]{1,0:T(8,128)(2,1)S(1)} %get-tuple-element.189), channel_id=1, source_target_pairs={{0,2},{1,3},{2,0},{3,1},{4,6},{5,7},{6,4},{7,5},{8,10},{9,11},{10,... | collective-permute-start | bytes 221384 | tf_op jit(solution)/shard_map/ppermute | solution.py:66
  602.8 4.8 collective-permute-start.44
  (216 other events, 1452.0 us)
Sparse Core Ops, SparseCore 0:
  32.3 59.0 all-gather.2
  93.6 89.9 all-gather.4
  379.0 69.2 reduce-scatter.9
  452.2 73.2 reduce-scatter.13
  529.2 69.6 reduce-scatter.11
